TPU v7x, 32 devices: a whole 2x2x4 slice. The times are simulated.
32 devices in a mesh: grp: 2 (over y), row: 4 (over z), col: 2 (over x), rep: 2 (over core).
Axes of the slice: x: 2, y: 2, z: 4, core: 2. Of those that a mesh axis runs over, the one named last changes fastest.
Arguments:
- h_strips: bfloat16 [64, 64, 1024], P(('grp', 'row')), parts along dimension 0, may hold values from -0.1875 to 0.1875
- h_slots: int32 [64, 16], P(('grp', 'row')), parts along dimension 0, may hold values from 0 to 23, all different within a row
- t_prev: float32 [4096, 2048], P(('grp', 'row'), ('col', 'rep')), parts along dimension 0, may hold values from -6 to 6
- t_now: float32 [4096, 2048], P(('grp', 'row'), ('col', 'rep')), parts along dimension 0, may hold values from -6 to 6
- t_mask: int32 [64, 32], P(('grp', 'row'), ('col', 'rep')), parts along dimension 0, may hold values 0 or 1
- coeffs: float32 [2], replicated, may hold values from 0.5 to 1.5
Outputs:
- t_mid: float32 [4096, 2048], P(('grp', 'row'), ('col', 'rep')), parts along dimension 0
- t_next: float32 [4096, 2048], P(('grp', 'row'), ('col', 'rep')), parts along dimension 0
- density: float32 [4096, 2048], P(('grp', 'row'), ('col', 'rep')), parts along dimension 0
There are 2 independent parts, one for each index of `grp`. A program takes and returns all parts, laid end to end along the dimension named above; an argument that names none is the same for every part. Nothing has to cross between parts.
Inputs may be any that keep to these rules, and one draw needn't show every extreme that they name: `h_slots`: in each block row the 16 values are distinct.
All inputs are finite; a program needn't handle non-finite values. No bound on the sum of `t_mask` on one device may be relied on, other than what follows from the above.
Results may differ from a plain program's by a relative error of at most 0.0037.
Values may be sent and summed in bfloat16 or wider, within the bound.
No kernel may reach another device: no remote copies, remote signals or barrier semaphores. Data moves between devices by JAX's collectives and lax.ppermute only.
A program may use at most 64 MiB of HBM per device.

v0:
```python
import functools

import jax
import jax.numpy as jnp
from jax import lax
from jax.experimental import pallas as pl
from jax.experimental.pallas import tpu as pltpu
from jax.sharding import PartitionSpec as P

LANES = 128
CHUNKS = 4
MIB = 1024 * 1024

SMEM = pl.BlockSpec(memory_space=pltpu.SMEM)
VMEM = pl.BlockSpec(memory_space=pltpu.VMEM)
HBM = pl.BlockSpec(memory_space=pltpu.HBM)


def spans_of(columns):
    width = columns // 2 if columns % (2 * LANES) == 0 else LANES
    return [(start, width) for start in range(0, columns, width)]


def both_sides(block):
    rows, reps = lax.axis_size("row"), lax.axis_size("rep")
    arrived = []
    for turn in (1, -1):
        route = []
        for row in range(rows):
            for rep in range(reps):
                source = (row + (turn if rep % 2 == 0 else -turn)) % rows
                route.append((source * reps + rep, row * reps + rep))
        arrived.append(lax.ppermute(block, ("row", "rep"), route))
    return tuple(arrived)


def side_columns(depth, order):
    odd = lax.axis_index("rep") % 2
    return pl.ds(pl.multiple_of(jnp.where(odd == order, 2 * depth, 0), LANES), depth)


def params(limit=32 * MIB):
    return pltpu.CompilerParams(vmem_limit_bytes=limit)


def cost(flops, moved):
    return pl.CostEstimate(flops=flops, transcendentals=0, bytes_accessed=moved)


def round_kernel(starts, now_ref, *out_refs):
    for start, out_ref in zip(starts, out_refs):
        out_ref[...] = now_ref[:, start:start + out_ref.shape[1]].astype(jnp.bfloat16)


def rounded(now, spans):
    rows = now.shape[0]
    size = rows * sum(width for _, width in spans)
    return list(pl.pallas_call(
        functools.partial(round_kernel, [start for start, _ in spans]),
        in_specs=[VMEM],
        out_specs=[VMEM] * len(spans),
        out_shape=[jax.ShapeDtypeStruct((rows, width), jnp.bfloat16) for _, width in spans],
        compiler_params=params(),
        cost_estimate=cost(size, 6 * size),
        name="round_part",
    )(now))


def band_kernel(slots_ref, strips_ref, out_ref):
    block_rows, block, slot_lanes = strips_ref.shape
    out_ref[...] = jnp.zeros_like(out_ref)
    half = lax.broadcasted_iota(jnp.int32, (block, LANES), 1) // block

    @pl.loop(0, block_rows)
    def _(row):
        at = pl.ds(pl.multiple_of(row * block, block), block)
        for pair in range(slot_lanes // LANES):
            straight = strips_ref[row, :, pair * LANES:(pair + 1) * LANES].astype(jnp.float32)
            swapped = jnp.concatenate([straight[:, block:], straight[:, :block]], axis=1)
            for side in range(2):
                target = slots_ref[row, 2 * pair + side]
                odd = target % 2
                value = jnp.where(odd == side, straight, swapped)
                value = jnp.where(half == odd, value, 0.0).astype(jnp.bfloat16)
                lanes = pl.ds(pl.multiple_of((target // 2) * LANES, LANES), LANES)
                out_ref[at, lanes] += value


def banded(h_slots, h_strips):
    block_rows, block, slot_lanes = h_strips.shape
    rows, columns = block_rows * block, 3 * block_rows * block
    return pl.pallas_call(
        band_kernel,
        in_specs=[SMEM, VMEM],
        out_specs=VMEM,
        out_shape=jax.ShapeDtypeStruct((rows, columns), jnp.bfloat16),
        compiler_params=params(),
        cost_estimate=cost(8 * rows * columns, 2 * rows * (columns + slot_lanes)),
        name="band",
    )(h_slots, h_strips)


def begun_product(band_ref, here_ref, first_ref):
    depth = here_ref.shape[0]
    total = jnp.dot(band_ref[:, depth:2 * depth], here_ref[...], preferred_element_type=jnp.float32)
    total += jnp.dot(band_ref[:, side_columns(depth, 0)], first_ref[...], preferred_element_type=jnp.float32)
    return total


def kept(mask_ref, block_row, first, block, width):
    column = lax.broadcasted_iota(jnp.int32, (block, width), 1) // block
    row = jnp.zeros((block, width), jnp.int32)
    for c in range(width // block):
        row = jnp.where(column == c, mask_ref[block_row, first + c], row)
    return row != 0


def mid_kernel(start, mask_ref, coeffs_ref, band_ref, here_ref, first_ref, second_ref, prev_ref, *rest):
    mid_ref, round_ref, share_ref, held, sems = rest[-5:]
    rows, width = here_ref.shape
    block = rows // mask_ref.shape[0]
    columns = slice(start, start + width)
    total = begun_product(band_ref, here_ref, first_ref)
    total += jnp.dot(band_ref[:, side_columns(rows, 1)], second_ref[...], preferred_element_type=jnp.float32)
    step = rows // CHUNKS
    copies = []
    for i in range(rows // block):
        at = slice(i * block, (i + 1) * block)
        keep = kept(mask_ref, i, start // block, block, width)
        value = jnp.where(keep, 2.0 * total[at] - prev_ref[at, columns], 0.0)
        held[at, :] = value
        round_ref[at, :] = value.astype(jnp.bfloat16)
        share_ref[at, :] = coeffs_ref[0] * value
        if (i + 1) * block % step == 0:
            c = len(copies)
            done = pl.ds(c * step, step)
            copies.append(pltpu.make_async_copy(
                held.at[done, :], mid_ref.at[done, pl.ds(start, width)], sems.at[c]))
            copies[-1].start()
    for copy in copies:
        copy.wait()


def mid_part(span, mask, coeffs, band, here, first, second, prev, mid):
    rows, width = here.shape
    operands = [mask, coeffs, band, here, first, second, prev]
    specs = [SMEM] * 2 + [VMEM] * 5
    aliases = {}
    if mid is not None:
        aliases = {len(operands): 0}
        operands.append(mid)
        specs.append(HBM)
    return pl.pallas_call(
        functools.partial(mid_kernel, span[0]),
        in_specs=specs,
        out_specs=[HBM, VMEM, VMEM],
        out_shape=[
            jax.ShapeDtypeStruct(prev.shape, jnp.float32),
            jax.ShapeDtypeStruct((rows, width), jnp.bfloat16),
            jax.ShapeDtypeStruct((rows, width), jnp.float32),
        ],
        scratch_shapes=[pltpu.VMEM((rows, width), jnp.float32), pltpu.SemaphoreType.DMA((CHUNKS,))],
        input_output_aliases=aliases,
        compiler_params=params(),
        cost_estimate=cost(6 * rows * rows * width, 6 * rows * rows + 20 * rows * width),
        name="mid_part",
    )(*operands)


def begun_kernel(start, band_ref, here_ref, first_ref, now_ref, sums_ref):
    width = here_ref.shape[1]
    total = begun_product(band_ref, here_ref, first_ref)
    sums_ref[...] = 2.0 * total - now_ref[:, start:start + width]


def begun_part(span, band, here, first, now):
    rows, width = here.shape
    return pl.pallas_call(
        functools.partial(begun_kernel, span[0]),
        in_specs=[VMEM] * 4,
        out_specs=VMEM,
        out_shape=jax.ShapeDtypeStruct((rows, width), jnp.float32),
        compiler_params=params(),
        cost_estimate=cost(4 * rows * rows * width, 4 * rows * rows + 12 * rows * width),
        name="next_begun",
    )(band, here, first, now)


def next_kernel(start, mask_ref, coeffs_ref, band_ref, second_ref, sums_ref, share_ref, *rest):
    next_ref, density_ref, held_next, held_density, sems = rest[-5:]
    rows, width = second_ref.shape
    block = rows // mask_ref.shape[0]
    step = rows // CHUNKS
    copies = []
    for c in range(CHUNKS):
        total = jnp.dot(
            band_ref[c * step:(c + 1) * step, side_columns(rows, 1)], second_ref[...], preferred_element_type=jnp.float32)
        for i in range(step // block):
            at = slice(c * step + i * block, c * step + (i + 1) * block)
            keep = kept(mask_ref, c * (step // block) + i, start // block, block, width)
            value = jnp.where(keep, 2.0 * total[i * block:(i + 1) * block] + sums_ref[at, :], 0.0)
            held_next[at, :] = value
            held_density[at, :] = share_ref[at, :] + coeffs_ref[1] * value
        done = pl.ds(c * step, step)
        for held, out_ref in ((held_next, next_ref), (held_density, density_ref)):
            copies.append(pltpu.make_async_copy(
                held.at[done, :], out_ref.at[done, pl.ds(start, width)], sems.at[len(copies)]))
            copies[-1].start()
    for copy in copies:
        copy.wait()


def next_part(span, mask, coeffs, band, second, sums, share, whole, outs):
    rows, width = second.shape
    operands = [mask, coeffs, band, second, sums, share]
    specs = [SMEM] * 2 + [VMEM] * 4
    aliases = {}
    if outs is not None:
        aliases = {len(operands): 0, len(operands) + 1: 1}
        operands += list(outs)
        specs += [HBM] * 2
    return pl.pallas_call(
        functools.partial(next_kernel, span[0]),
        in_specs=specs,
        out_specs=[HBM] * 2,
        out_shape=[jax.ShapeDtypeStruct(whole, jnp.float32)] * 2,
        scratch_shapes=[pltpu.VMEM((rows, width), jnp.float32)] * 2 + [pltpu.SemaphoreType.DMA((2 * CHUNKS,))],
        input_output_aliases=aliases,
        compiler_params=params(),
        cost_estimate=cost(2 * rows * rows * width, 2 * rows * rows + 22 * rows * width),
        name="next_part",
    )(*operands)


def local(h_strips, h_slots, t_prev, t_now, t_mask, coeffs):
    spans = spans_of(t_now.shape[1])
    parts = len(spans)
    start, width = spans[0]
    here = [t_now[:, start:start + width].astype(jnp.bfloat16)]
    here[0], t_now, t_prev, h_strips = lax.optimization_barrier((here[0], t_now, t_prev, h_strips))
    here += rounded(t_now, spans[1:])
    band = banded(h_slots, h_strips)
    sides = [both_sides(block) for block in here]
    mid, here_mid, shares, sides_mid = None, [], [], []
    for part in range(parts):
        mid, low, share = mid_part(spans[part], t_mask, coeffs, band, here[part], *sides[part], t_prev, mid)
        here_mid.append(low)
        shares.append(share)
        sides_mid.append(both_sides(low))
    outs = None
    for part in range(parts):
        first, second = sides_mid[part]
        sums = begun_part(spans[part], band, here_mid[part], first, t_now)
        outs = next_part(spans[part], t_mask, coeffs, band, second, sums, shares[part], t_now.shape, outs)
    return (mid, outs[0], outs[1])


def solution(mesh):
    panel = P(("grp", "row"), ("col", "rep"))
    return jax.shard_map(
        local,
        mesh=mesh,
        in_specs=(P(("grp", "row"), None, None), P(("grp", "row"), None), panel, panel, panel, P()),
        out_specs=(panel, panel, panel),
        check_vma=False,
    )
```

profile of v0, /device:TPU:0, one launch (start us, length us, event | category | flops | bytes accessed | tf_op | source)
XLA Modules:
  0.0 54.6 jit_solution(7090123580562957618)
XLA Ops:
  0.6 0.0 copy-start.6
  0.6 1.1 %slice.7.here_ref = bf16[512,256]{1,0:T(8,128)(2,1)S(1)} slice(f32[512,512]{1,0:T(8,128)} %now_ref.2), slice={[0:512], [0:256]} | slice | bytes 524288 | tf_op jit(solution)/shard_map/slice | solution.py:239
  1.7 3.1 %collective-permute-start.3 = (bf16[512,256]{1,0:T(8,128)(2,1)S(1)}, bf16[512,256]{1,0:T(8,128)(2,1)S(1)}, u32[]{:S(2)}, u32[]{:S(2)}) collective-permute-start(bf16[512,256]{1,0:T(8,128)(2,1)S(1)} %slice.7.here_ref), channel_id=1, source_target_pairs={{12,0},{5,1},{0,4},{9,5},{4,8},{13,9},{8,12},{1,13},{14,2},{7,3},{... | collective-permute-start | bytes 786440 | tf_op jit(solution)/shard_map/ppermute | solution.py:33
  4.8 2.1 %collective-permute-start.2 = (bf16[512,256]{1,0:T(8,128)(2,1)S(1)}, bf16[512,256]{1,0:T(8,128)(2,1)S(1)}, u32[]{:S(2)}, u32[]{:S(2)}) collective-permute-start(bf16[512,256]{1,0:T(8,128)(2,1)S(1)} %slice.7.here_ref), channel_id=1, source_target_pairs={{4,0},{13,1},{8,4},{1,5},{12,8},{5,9},{0,12},{9,13},{6,2},{15,3},{... | collective-permute-start | bytes 786440 | tf_op jit(solution)/shard_map/ppermute | solution.py:33
  6.9 0.0 copy-start
  6.9 1.2 %copy-done = f32[512,512]{1,0:T(8,128)S(1)} copy-done((f32[512,512]{1,0:T(8,128)S(1)}, f32[512,512]{1,0:T(8,128)}, u32[]{:S(2)}) %copy-start) | copy-done | bytes 1048600
  8.1 0.0 copy-start.3
  8.2 0.0 copy-start.2
  8.2 0.0 copy-start.4
  8.2 0.0 copy-start.5
  8.2 0.1 collective-permute-start.1
  8.3 3.8 %collective-permute-start = (bf16[512,256]{1,0:T(8,128)(2,1)S(1)}, bf16[512,256]{1,0:T(8,128)(2,1)S(1)}, u32[]{:S(2)}, u32[]{:S(2)}) collective-permute-start(bf16[512,256]{1,0:T(8,128)(2,1)S(1)} %round_part.1.here_ref), channel_id=1, source_target_pairs={{4,0},{13,1},{8,4},{1,5},{12,8},{5,9},{0,12},{9,13},{6,2},{15,3},{... | collective-permute-start | bytes 786440 | tf_op jit(solution)/shard_map/ppermute | solution.py:33
  12.1 0.0 copy-done.6
  12.1 0.0 copy-done.3
  12.1 2.2 %band.1.band_ref = bf16[512,1536]{1,0:T(8,128)(2,1)S(1)} custom-call(s32[8,16]{1,0:T(8,128)S(1)} %copy-done.6, bf16[8,64,1024]{2,1,0:T(8,128)(2,1)S(1)} %copy-done.3), custom_call_target="tpu_custom_call" | custom-call | flops 6291456 | bytes 2621440 | tf_op jit(solution)/shard_map/band/pallas_call | solution.py:92
  14.2 0.0 collective-permute-done.3.second_ref
  14.3 4.3 %collective-permute-done.2.first_ref = bf16[512,256]{1,0:T(8,128)(2,1)S(1)} collective-permute-done((bf16[512,256]{1,0:T(8,128)(2,1)S(1)}, bf16[512,256]{1,0:T(8,128)(2,1)S(1)}, u32[]{:S(2)}, u32[]{:S(2)}) %collective-permute-start.2) | collective-permute-done | bytes 262176 | tf_op jit(solution)/shard_map/ppermute | solution.py:33
  18.6 0.0 copy-done.2
  18.6 0.0 copy-done.4
  18.6 0.0 copy-done.5
  18.6 1.9 %mid_part.2 = (f32[512,512]{1,0:T(8,128)}, bf16[512,256]{1,0:T(8,128)(2,1)S(1)}, f32[512,256]{1,0:T(8,128)S(1)}) custom-call(s32[8,8]{1,0:T(8,128)S(1)} %copy-done.4, f32[2]{0:T(128)S(1)} %copy-done.5, bf16[512,1536]{1,0:T(8,128)(2,1)S(1)} %band.1.band_ref, bf16[512,256]{1,0:T(8,128)(2,1)S(1)} %slice.7.here_ref, ...), custom_call_target="tpu_custom_call" | custom-call | flops 402653184 | bytes 4194304 | tf_op jit(solution)/shard_map/mid_part/pallas_call | solution.py:153
  20.5 3.1 %collective-permute-start.7 = (bf16[512,256]{1,0:T(8,128)(2,1)S(1)}, bf16[512,256]{1,0:T(8,128)(2,1)S(1)}, u32[]{:S(2)}, u32[]{:S(2)}) collective-permute-start(bf16[512,256]{1,0:T(8,128)(2,1)S(1)} %get-tuple-element.25.here_ref), channel_id=1, source_target_pairs={{4,0},{13,1},{8,4},{1,5},{12,8},{5,9},{0,12},{9,13},{6,2},{15,3},{... | collective-permute-start | bytes 786440 | tf_op jit(solution)/shard_map/ppermute | solution.py:33
  23.6 0.0 collective-permute-start.6
  23.6 1.7 %collective-permute-done.1.second_ref = bf16[512,256]{1,0:T(8,128)(2,1)S(1)} collective-permute-done((bf16[512,256]{1,0:T(8,128)(2,1)S(1)}, bf16[512,256]{1,0:T(8,128)(2,1)S(1)}, u32[]{:S(2)}, u32[]{:S(2)}) %collective-permute-start.1) | collective-permute-done | bytes 262176 | tf_op jit(solution)/shard_map/ppermute | solution.py:33
  25.3 2.2 %collective-permute-done.first_ref = bf16[512,256]{1,0:T(8,128)(2,1)S(1)} collective-permute-done((bf16[512,256]{1,0:T(8,128)(2,1)S(1)}, bf16[512,256]{1,0:T(8,128)(2,1)S(1)}, u32[]{:S(2)}, u32[]{:S(2)}) %collective-permute-start) | collective-permute-done | bytes 262176 | tf_op jit(solution)/shard_map/ppermute | solution.py:33
  27.5 0.0 copy-start.1
  27.5 1.9 %mid_part.3 = (f32[512,512]{1,0:T(8,128)}, bf16[512,256]{1,0:T(8,128)(2,1)S(1)}, f32[512,256]{1,0:T(8,128)S(1)}) custom-call(s32[8,8]{1,0:T(8,128)S(1)} %copy-done.4, f32[2]{0:T(128)S(1)} %copy-done.5, bf16[512,1536]{1,0:T(8,128)(2,1)S(1)} %band.1.band_ref, bf16[512,256]{1,0:T(8,128)(2,1)S(1)} %round_part.1.here_ref, ...), custom_call_target="tpu_custom_call", output_to_operand_aliasing={{0}: (7, {})} | custom-call | flops 402653184 | bytes 4194304 | tf_op jit(solution)/shard_map/mid_part/pallas_call | solution.py:153
  29.4 6.4 %collective-permute-start.5 = (bf16[512,256]{1,0:T(8,128)(2,1)S(1)}, bf16[512,256]{1,0:T(8,128)(2,1)S(1)}, u32[]{:S(2)}, u32[]{:S(2)}) collective-permute-start(bf16[512,256]{1,0:T(8,128)(2,1)S(1)} %get-tuple-element.23.here_ref), channel_id=1, source_target_pairs={{4,0},{13,1},{8,4},{1,5},{12,8},{5,9},{0,12},{9,13},{6,2},{15,3},{... | collective-permute-start | bytes 786440 | tf_op jit(solution)/shard_map/ppermute | solution.py:33
  35.8 0.0 collective-permute-start.4
  35.8 1.1 %collective-permute-done.7.first_ref = bf16[512,256]{1,0:T(8,128)(2,1)S(1)} collective-permute-done((bf16[512,256]{1,0:T(8,128)(2,1)S(1)}, bf16[512,256]{1,0:T(8,128)(2,1)S(1)}, u32[]{:S(2)}, u32[]{:S(2)}) %collective-permute-start.7) | collective-permute-done | bytes 262176 | tf_op jit(solution)/shard_map/ppermute | solution.py:33
  36.9 0.0 copy-done.1
  36.9 0.4 next_begun.3.sums_ref
  37.4 4.9 %collective-permute-done.6.second_ref = bf16[512,256]{1,0:T(8,128)(2,1)S(1)} collective-permute-done((bf16[512,256]{1,0:T(8,128)(2,1)S(1)}, bf16[512,256]{1,0:T(8,128)(2,1)S(1)}, u32[]{:S(2)}, u32[]{:S(2)}) %collective-permute-start.6) | collective-permute-done | bytes 262176 | tf_op jit(solution)/shard_map/ppermute | solution.py:33
  42.2 1.9 %next_part.2 = (f32[512,512]{1,0:T(8,128)}, f32[512,512]{1,0:T(8,128)}) custom-call(s32[8,8]{1,0:T(8,128)S(1)} %copy-done.4, f32[2]{0:T(128)S(1)} %copy-done.5, bf16[512,1536]{1,0:T(8,128)(2,1)S(1)} %band.1.band_ref, bf16[512,256]{1,0:T(8,128)(2,1)S(1)} %collective-permute-done.6.second_ref, f32[512,256]{1,0:T(8,128)S(1)} %next_begun.3.sums_ref, ...), custom_call_target="tpu_custom_call" | custom-call | flops 134217728 | bytes 3407872 | tf_op jit(solution)/shard_map/next_part/pallas_call | solution.py:222
  44.1 3.6 %collective-permute-done.5.first_ref = bf16[512,256]{1,0:T(8,128)(2,1)S(1)} collective-permute-done((bf16[512,256]{1,0:T(8,128)(2,1)S(1)}, bf16[512,256]{1,0:T(8,128)(2,1)S(1)}, u32[]{:S(2)}, u32[]{:S(2)}) %collective-permute-start.5) | collective-permute-done | bytes 262176 | tf_op jit(solution)/shard_map/ppermute | solution.py:33
  47.7 0.4 next_begun.2.sums_ref
  48.1 4.6 %collective-permute-done.4.second_ref = bf16[512,256]{1,0:T(8,128)(2,1)S(1)} collective-permute-done((bf16[512,256]{1,0:T(8,128)(2,1)S(1)}, bf16[512,256]{1,0:T(8,128)(2,1)S(1)}, u32[]{:S(2)}, u32[]{:S(2)}) %collective-permute-start.4) | collective-permute-done | bytes 262176 | tf_op jit(solution)/shard_map/ppermute | solution.py:33
  52.7 1.9 %next_part.3 = (f32[512,512]{1,0:T(8,128)}, f32[512,512]{1,0:T(8,128)}) custom-call(s32[8,8]{1,0:T(8,128)S(1)} %copy-done.4, f32[2]{0:T(128)S(1)} %copy-done.5, bf16[512,1536]{1,0:T(8,128)(2,1)S(1)} %band.1.band_ref, bf16[512,256]{1,0:T(8,128)(2,1)S(1)} %collective-permute-done.4.second_ref, ...), custom_call_target="tpu_custom_call", output_to_operand_aliasing={{0}: (6, {}), {1}: (7, {})} | custom-call | flops 134217728 | bytes 3407872 | tf_op jit(solution)/shard_map/next_part/pallas_call | solution.py:222
  (1 shorter events, 0.0 us)
Async XLA Ops:
  0.6 11.4 %copy-start.6 = (s32[8,16]{1,0:T(8,128)S(1)}, s32[8,16]{1,0:T(8,128)}, u32[]{:S(2)}) copy-start(s32[8,16]{1,0:T(8,128)} %slots_ref.1) | copy-start | bytes 1540
  1.7 12.5 %collective-permute-start.3 = (bf16[512,256]{1,0:T(8,128)(2,1)S(1)}, bf16[512,256]{1,0:T(8,128)(2,1)S(1)}, u32[]{:S(2)}, u32[]{:S(2)}) collective-permute-start(bf16[512,256]{1,0:T(8,128)(2,1)S(1)} %slice.7.here_ref), channel_id=1, source_target_pairs={{12,0},{5,1},{0,4},{9,5},{4,8},{13,9},{8,12},{1,13},{14,2},{7,3},{... | collective-permute-start | bytes 786440 | tf_op jit(solution)/shard_map/ppermute | solution.py:33
  4.8 13.8 %collective-permute-start.2 = (bf16[512,256]{1,0:T(8,128)(2,1)S(1)}, bf16[512,256]{1,0:T(8,128)(2,1)S(1)}, u32[]{:S(2)}, u32[]{:S(2)}) collective-permute-start(bf16[512,256]{1,0:T(8,128)(2,1)S(1)} %slice.7.here_ref), channel_id=1, source_target_pairs={{4,0},{13,1},{8,4},{1,5},{12,8},{5,9},{0,12},{9,13},{6,2},{15,3},{... | collective-permute-start | bytes 786440 | tf_op jit(solution)/shard_map/ppermute | solution.py:33
  6.9 1.2 %copy-start = (f32[512,512]{1,0:T(8,128)S(1)}, f32[512,512]{1,0:T(8,128)}, u32[]{:S(2)}) copy-start(f32[512,512]{1,0:T(8,128)} %now_ref.2) | copy-start | bytes 3145732
  8.1 4.0 %copy-start.3 = (bf16[8,64,1024]{2,1,0:T(8,128)(2,1)S(1)}, bf16[8,64,1024]{2,1,0:T(8,128)(2,1)}, u32[]{:S(2)}) copy-start(bf16[8,64,1024]{2,1,0:T(8,128)(2,1)} %strips_ref) | copy-start | bytes 3145732
  8.2 10.4 %copy-start.2 = (f32[512,512]{1,0:T(8,128)S(1)}, f32[512,512]{1,0:T(8,128)}, u32[]{:S(2)}) copy-start(f32[512,512]{1,0:T(8,128)} %prev_ref.1) | copy-start | bytes 3145732
  8.2 10.4 %copy-start.4 = (s32[8,8]{1,0:T(8,128)S(1)}, s32[8,8]{1,0:T(8,128)}, u32[]{:S(2)}) copy-start(s32[8,8]{1,0:T(8,128)} %mask_ref.7) | copy-start | bytes 772
  8.2 10.4 %copy-start.5 = (f32[2]{0:T(128)S(1)}, f32[2]{0:T(128)}, u32[]{:S(2)}) copy-start(f32[2]{0:T(128)} %coeffs_ref.7) | copy-start | bytes 28
  8.2 17.1 %collective-permute-start.1 = (bf16[512,256]{1,0:T(8,128)(2,1)S(1)}, bf16[512,256]{1,0:T(8,128)(2,1)S(1)}, u32[]{:S(2)}, u32[]{:S(2)}) collective-permute-start(bf16[512,256]{1,0:T(8,128)(2,1)S(1)} %round_part.1.here_ref), channel_id=1, source_target_pairs={{12,0},{5,1},{0,4},{9,5},{4,8},{13,9},{8,12},{1,13},{14,2},{7,3},{... | collective-permute-start | bytes 786440 | tf_op jit(solution)/shard_map/ppermute | solution.py:33
  8.3 19.3 %collective-permute-start = (bf16[512,256]{1,0:T(8,128)(2,1)S(1)}, bf16[512,256]{1,0:T(8,128)(2,1)S(1)}, u32[]{:S(2)}, u32[]{:S(2)}) collective-permute-start(bf16[512,256]{1,0:T(8,128)(2,1)S(1)} %round_part.1.here_ref), channel_id=1, source_target_pairs={{4,0},{13,1},{8,4},{1,5},{12,8},{5,9},{0,12},{9,13},{6,2},{15,3},{... | collective-permute-start | bytes 786440 | tf_op jit(solution)/shard_map/ppermute | solution.py:33
  20.5 16.4 %collective-permute-start.7 = (bf16[512,256]{1,0:T(8,128)(2,1)S(1)}, bf16[512,256]{1,0:T(8,128)(2,1)S(1)}, u32[]{:S(2)}, u32[]{:S(2)}) collective-permute-start(bf16[512,256]{1,0:T(8,128)(2,1)S(1)} %get-tuple-element.25.here_ref), channel_id=1, source_target_pairs={{4,0},{13,1},{8,4},{1,5},{12,8},{5,9},{0,12},{9,13},{6,2},{15,3},{... | collective-permute-start | bytes 786440 | tf_op jit(solution)/shard_map/ppermute | solution.py:33
  23.6 18.6 %collective-permute-start.6 = (bf16[512,256]{1,0:T(8,128)(2,1)S(1)}, bf16[512,256]{1,0:T(8,128)(2,1)S(1)}, u32[]{:S(2)}, u32[]{:S(2)}) collective-permute-start(bf16[512,256]{1,0:T(8,128)(2,1)S(1)} %get-tuple-element.25.here_ref), channel_id=1, source_target_pairs={{12,0},{5,1},{0,4},{9,5},{4,8},{13,9},{8,12},{1,13},{14,2},{7,3},{... | collective-permute-start | bytes 786440 | tf_op jit(solution)/shard_map/ppermute | solution.py:33
  27.5 9.4 %copy-start.1 = (f32[512,512]{1,0:T(8,128)S(1)}, f32[512,512]{1,0:T(8,128)}, u32[]{:S(2)}) copy-start(f32[512,512]{1,0:T(8,128)} %now_ref.2) | copy-start | bytes 3145732
  29.4 18.3 %collective-permute-start.5 = (bf16[512,256]{1,0:T(8,128)(2,1)S(1)}, bf16[512,256]{1,0:T(8,128)(2,1)S(1)}, u32[]{:S(2)}, u32[]{:S(2)}) collective-permute-start(bf16[512,256]{1,0:T(8,128)(2,1)S(1)} %get-tuple-element.23.here_ref), channel_id=1, source_target_pairs={{4,0},{13,1},{8,4},{1,5},{12,8},{5,9},{0,12},{9,13},{6,2},{15,3},{... | collective-permute-start | bytes 786440 | tf_op jit(solution)/shard_map/ppermute | solution.py:33
  35.8 16.9 %collective-permute-start.4 = (bf16[512,256]{1,0:T(8,128)(2,1)S(1)}, bf16[512,256]{1,0:T(8,128)(2,1)S(1)}, u32[]{:S(2)}, u32[]{:S(2)}) collective-permute-start(bf16[512,256]{1,0:T(8,128)(2,1)S(1)} %get-tuple-element.23.here_ref), channel_id=1, source_target_pairs={{12,0},{5,1},{0,4},{9,5},{4,8},{13,9},{8,12},{1,13},{14,2},{7,3},{... | collective-permute-start | bytes 786440 | tf_op jit(solution)/shard_map/ppermute | solution.py:33
where the time goes:
time: 54.8 us; the launch traced here: 54.6 us
  waiting for transfers between devices  22.3 us (41%)
  starting transfers between devices  18.6 us (34%)
  Pallas kernels  10.6 us (19%)
  local copies, waits for them, and re-layouts  2.33 us (4%)
  between operations  0.75 us (1%)
    ppermute x8, waiting for transfers between devices, both_sides(): arrived.append(lax.ppermute(block, ('row', 'rep'), route))  22.3 us
    ppermute x8, starting transfers between devices, both_sides(): arrived.append(lax.ppermute(block, ('row', 'rep'), route))  18.6 us
    pallas_call x2, Pallas kernels, mid_part(): pl.pallas_call(functools.partial(mid_kernel, span[0]), in_specs=specs, ou...  3.8 us
    pallas_call x2, Pallas kernels, next_part(): pl.pallas_call(functools.partial(next_kernel, span[0]), in_specs=specs, o...  3.75 us
    pallas_call x1, Pallas kernels, banded(): pl.pallas_call(band_kernel, in_specs=[SMEM, VMEM], out_specs=VMEM, out_sh...  2.17 us
    unnamed x14, local copies, waits for them, and re-layouts  1.25 us
  transfers between devices with their start and end apart: 8, of which 7 were waited for; matrix products, arithmetic and copies ran while one was open for 0% of the time, Pallas kernels for 16%

commit v1 on v0

v1 whole, which is shorter than its diff:
```python
import functools

import jax
import jax.numpy as jnp
from jax import lax
from jax.experimental import pallas as pl
from jax.experimental.pallas import tpu as pltpu
from jax.sharding import PartitionSpec as P

LANES = 128
CHUNKS = 2
MIB = 1024 * 1024

SMEM = pl.BlockSpec(memory_space=pltpu.SMEM)
VMEM = pl.BlockSpec(memory_space=pltpu.VMEM)
ANY = pl.BlockSpec(memory_space=pl.ANY)
HBM = pl.BlockSpec(memory_space=pltpu.HBM)


def spans_of(columns):
    width = columns // 4 if columns % (4 * LANES) == 0 else LANES
    return [(start, width) for start in range(0, columns, width)]


def both_sides(block):
    rows = lax.axis_size("row")
    return tuple(
        lax.ppermute(block, "row", [((row - turn) % rows, row) for row in range(rows)]) for turn in (1, -1))


def side_columns(depth, order):
    return pl.ds(2 * depth * order, depth)


def params(limit=32 * MIB):
    return pltpu.CompilerParams(vmem_limit_bytes=limit)


def cost(flops, moved):
    return pl.CostEstimate(flops=flops, transcendentals=0, bytes_accessed=moved)


def round_kernel(starts, now_ref, *out_refs):
    for start, out_ref in zip(starts, out_refs):
        out_ref[...] = now_ref[:, start:start + out_ref.shape[1]].astype(jnp.bfloat16)


def rounded(now, spans):
    rows = now.shape[0]
    size = rows * sum(width for _, width in spans)
    return list(pl.pallas_call(
        functools.partial(round_kernel, [start for start, _ in spans]),
        in_specs=[VMEM],
        out_specs=[VMEM] * len(spans),
        out_shape=[jax.ShapeDtypeStruct((rows, width), jnp.bfloat16) for _, width in spans],
        compiler_params=params(),
        cost_estimate=cost(size, 6 * size),
        name="round_part",
    )(now))


def band_kernel(slots_ref, strips_ref, out_ref):
    block_rows, block, slot_lanes = strips_ref.shape
    out_ref[...] = jnp.zeros_like(out_ref)
    half = lax.broadcasted_iota(jnp.int32, (block, LANES), 1) // block

    @pl.loop(0, block_rows)
    def _(row):
        at = pl.ds(pl.multiple_of(row * block, block), block)
        for pair in range(slot_lanes // LANES):
            straight = strips_ref[row, :, pair * LANES:(pair + 1) * LANES].astype(jnp.float32)
            swapped = jnp.concatenate([straight[:, block:], straight[:, :block]], axis=1)
            for side in range(2):
                target = slots_ref[row, 2 * pair + side]
                odd = target % 2
                value = jnp.where(odd == side, straight, swapped)
                value = jnp.where(half == odd, value, 0.0).astype(jnp.bfloat16)
                lanes = pl.ds(pl.multiple_of((target // 2) * LANES, LANES), LANES)
                out_ref[at, lanes] += value


def banded(h_slots, h_strips):
    block_rows, block, slot_lanes = h_strips.shape
    rows, columns = block_rows * block, 3 * block_rows * block
    return pl.pallas_call(
        band_kernel,
        in_specs=[SMEM, VMEM],
        out_specs=VMEM,
        out_shape=jax.ShapeDtypeStruct((rows, columns), jnp.bfloat16),
        compiler_params=params(),
        cost_estimate=cost(8 * rows * columns, 2 * rows * (columns + slot_lanes)),
        name="band",
    )(h_slots, h_strips)


def product(band_ref, here_ref, first_ref, second_ref=None):
    depth = here_ref.shape[0]
    total = jnp.dot(band_ref[:, depth:2 * depth], here_ref[...], preferred_element_type=jnp.float32)
    total += jnp.dot(band_ref[:, side_columns(depth, 0)], first_ref[...], preferred_element_type=jnp.float32)
    if second_ref is not None:
        total += jnp.dot(band_ref[:, side_columns(depth, 1)], second_ref[...], preferred_element_type=jnp.float32)
    return total


def kept(mask_ref, block_row, first, block, width):
    column = lax.broadcasted_iota(jnp.int32, (block, width), 1) // block
    row = jnp.zeros((block, width), jnp.int32)
    for c in range(width // block):
        row = jnp.where(column == c, mask_ref[block_row, first + c], row)
    return row != 0


def masked(start, mask_ref, term):
    rows, width = term.shape
    block = rows // mask_ref.shape[0]
    for i in range(rows // block):
        at = slice(i * block, (i + 1) * block)
        yield at, jnp.where(kept(mask_ref, i, start // block, block, width), term[at], 0.0)


def writes(jobs, sems):
    copies = []
    for held, out_ref, start in jobs:
        columns = pl.ds(start, held.shape[1])
        copies.append(pltpu.make_async_copy(held, out_ref.at[:, columns], sems.at[len(copies)]))
        copies[-1].start()
    return copies


def mid_kernel(start, mask_ref, band_ref, here_ref, first_ref, second_ref, prev_ref, *rest):
    mid_ref, round_ref = rest[-2:]
    total = product(band_ref, here_ref, first_ref, second_ref)
    term = 2.0 * total - prev_ref[:, start:start + here_ref.shape[1]]
    for at, value in masked(start, mask_ref, term):
        mid_ref[at, :] = value
        round_ref[at, :] = value.astype(jnp.bfloat16)


def mid_part(span, mask, band, here, first, second, prev, after):
    rows, width = here.shape
    return pl.pallas_call(
        functools.partial(mid_kernel, span[0]),
        in_specs=[SMEM] + [VMEM] * 5 + [ANY] * len(after),
        out_specs=[VMEM] * 2,
        out_shape=[jax.ShapeDtypeStruct(here.shape, jnp.float32), jax.ShapeDtypeStruct(here.shape, jnp.bfloat16)],
        compiler_params=params(),
        cost_estimate=cost(6 * rows * rows * width, 6 * rows * rows + 16 * rows * width),
        name="mid_part",
    )(mask, band, here, first, second, prev, *after)


def next_kernel(start, places, panels, unread, mask_ref, coeffs_ref, band_ref, here_ref, first_ref, second_ref, now_ref,
                mid_ref, *rest):
    rest = rest[unread:]
    held_refs, rest = rest[:len(places)], rest[len(places):]
    next_ref, density_ref, sems = rest[-panels - 3], rest[-panels - 2], rest[-1]
    out_refs = rest[-panels - 1:-1]
    copies = writes([(held, out_refs[o], at) for held, (o, at) in zip(held_refs, places)], sems)
    total = product(band_ref, here_ref, first_ref, second_ref)
    term = 2.0 * total - now_ref[:, start:start + here_ref.shape[1]]
    for at, value in masked(start, mask_ref, term):
        next_ref[at, :] = value
        density_ref[at, :] = coeffs_ref[0] * mid_ref[at, :] + coeffs_ref[1] * value
    for copy in copies:
        copy.wait()


def begun_kernel(start, places, panels, band_ref, here_ref, first_ref, now_ref, *rest):
    held_refs, rest = rest[:len(places)], rest[len(places):]
    sums_ref, sems = rest[-panels - 2], rest[-1]
    out_refs = rest[-panels - 1:-1]
    copies = writes([(held, out_refs[o], at) for held, (o, at) in zip(held_refs, places)], sems)
    sums_ref[...] = 2.0 * product(band_ref, here_ref, first_ref) - now_ref[:, start:start + here_ref.shape[1]]
    for copy in copies:
        copy.wait()


def with_writes(kernel, specs, operands, out_shapes, moves, panels, whole, outs, flops, name):
    held = [part for part, _ in moves]
    places = [place for _, place in moves]
    moved = sum(part.size for part in held)
    aliases = {}
    operands, specs = operands + held, specs + [VMEM] * len(held)
    if outs is not None:
        aliases = {len(operands) + o: len(out_shapes) + o for o in range(panels)}
        operands, specs = operands + list(outs), specs + [HBM] * panels
    results = pl.pallas_call(
        functools.partial(kernel, places),
        in_specs=specs,
        out_specs=[VMEM] * len(out_shapes) + [HBM] * panels,
        out_shape=out_shapes + [jax.ShapeDtypeStruct(whole, jnp.float32)] * panels,
        scratch_shapes=[pltpu.SemaphoreType.DMA((max(len(held), 1),))],
        input_output_aliases=aliases,
        compiler_params=params(),
        cost_estimate=cost(flops, 4 * moved + flops // 200),
        name=name,
    )(*operands)
    return results[:len(out_shapes)], tuple(results[len(out_shapes):])


def next_part(span, mask, coeffs, band, here, first, second, now, mid, after, moves, panels):
    rows, width = here.shape
    return with_writes(
        lambda places, *refs: next_kernel(span[0], places, panels, len(after), *refs),
        [SMEM] * 2 + [VMEM] * 6 + [ANY] * len(after), [mask, coeffs, band, here, first, second, now, mid, *after],
        [jax.ShapeDtypeStruct(here.shape, jnp.float32)] * 2, moves, panels, now.shape, None,
        6 * rows * rows * width, "next_part")


def begun_part(span, band, here, first, now, moves, panels, outs):
    rows, width = here.shape
    (sums,), outs = with_writes(
        lambda places, *refs: begun_kernel(span[0], places, panels, *refs),
        [VMEM] * 4, [band, here, first, now],
        [jax.ShapeDtypeStruct(here.shape, jnp.float32)], moves, panels, now.shape, outs,
        4 * rows * rows * width, "begun_part")
    return sums, outs


def last_kernel(start, mask_ref, coeffs_ref, band_ref, second_ref, sums_ref, mid_ref, *rest):
    next_ref, density_ref, held_next, held_density, sems = rest[-5:]
    rows, width = second_ref.shape
    block = rows // mask_ref.shape[0]
    step = rows // CHUNKS
    copies = []
    for c in range(CHUNKS):
        total = jnp.dot(
            band_ref[c * step:(c + 1) * step, side_columns(rows, 1)], second_ref[...],
            preferred_element_type=jnp.float32)
        for i in range(step // block):
            at = slice(c * step + i * block, c * step + (i + 1) * block)
            keep = kept(mask_ref, c * (step // block) + i, start // block, block, width)
            value = jnp.where(keep, 2.0 * total[i * block:(i + 1) * block] + sums_ref[at, :], 0.0)
            held_next[at, :] = value
            held_density[at, :] = coeffs_ref[0] * mid_ref[at, :] + coeffs_ref[1] * value
        done = pl.ds(c * step, step)
        for held, out_ref in ((held_next, next_ref), (held_density, density_ref)):
            copies.append(pltpu.make_async_copy(
                held.at[done, :], out_ref.at[done, pl.ds(start, width)], sems.at[len(copies)]))
            copies[-1].start()
    for copy in copies:
        copy.wait()


def last_part(span, mask, coeffs, band, second, sums, mid, outs):
    rows, width = second.shape
    return pl.pallas_call(
        functools.partial(last_kernel, span[0]),
        in_specs=[SMEM] * 2 + [VMEM] * 4 + [HBM] * 2,
        out_specs=[HBM] * 2,
        out_shape=[jax.ShapeDtypeStruct(out.shape, jnp.float32) for out in outs],
        scratch_shapes=[pltpu.VMEM((rows, width), jnp.float32)] * 2 + [pltpu.SemaphoreType.DMA((2 * CHUNKS,))],
        input_output_aliases={6: 0, 7: 1},
        compiler_params=params(),
        cost_estimate=cost(2 * rows * rows * width, 2 * rows * rows + 22 * rows * width),
        name="last_part",
    )(mask, coeffs, band, second, sums, mid, *outs)


def local(h_strips, h_slots, t_prev, t_now, t_mask, coeffs):
    spans = spans_of(t_now.shape[1])
    parts = len(spans)
    start, width = spans[0]
    here = [t_now[:, start:start + width].astype(jnp.bfloat16)]
    here[0], t_now, t_prev, h_strips = lax.optimization_barrier((here[0], t_now, t_prev, h_strips))
    here += rounded(t_now, spans[1:])
    band = banded(h_slots, h_strips)
    sides = [both_sides(block) for block in here]
    mids, here_mid, sides_mid = [], [], []
    for part in range(parts):
        first, second = sides[part]
        mid, low = mid_part(spans[part], t_mask, band, here[part], first, second, t_prev, mids[-1:])
        mids.append(mid)
        here_mid.append(low)
        sides_mid.append(both_sides(low))
    t_mid, outs, waiting, after = None, None, [], []
    for part in range(parts - 1):
        panels, moves = 0, []
        if part == 0:
            panels, moves = 1, [(mids[p], (0, spans[p][0])) for p in range(parts)]
        elif part == parts - 2:
            panels, moves = 2, waiting
        (term, density), written = next_part(
            spans[part], t_mask, coeffs, band, here_mid[part], *sides_mid[part], t_now, mids[part], after, moves, panels)
        after = [term]
        if part == 0:
            t_mid = written[0]
        elif part == parts - 2:
            outs, waiting = written, []
        waiting += [(term, (0, spans[part][0])), (density, (1, spans[part][0]))]
    first, second = sides_mid[-1]
    sums, outs = begun_part(spans[-1], band, here_mid[-1], first, t_now, waiting, 2, outs)
    outs = last_part(spans[-1], t_mask, coeffs, band, second, sums, mids[-1], outs)
    return (t_mid, outs[0], outs[1])


def solution(mesh):
    panel = P(("grp", "row"), ("col", "rep"))
    return jax.shard_map(
        local,
        mesh=mesh,
        in_specs=(P(("grp", "row"), None, None), P(("grp", "row"), None), panel, panel, panel, P()),
        out_specs=(panel, panel, panel),
        check_vma=False,
    )
```

time: 54.8 us -> 53.7 us (0.980)
  waiting for transfers between devices: 22.3 us -> 2.81 us
  starting transfers between devices: 18.6 us -> 31.9 us
  Pallas kernels: 10.6 us -> 15 us
  local copies, waits for them, and re-layouts: 2.33 us -> 2.9 us
    ppermute x8 -> x16, waiting for transfers between devices: 22.3 us -> 2.81 us  [both_sides(): lax.ppermute(block, 'row', [((row - turn) % rows, row) for row in range(r...]
    ppermute x8 -> x16, starting transfers between devices: 18.6 us -> 31.9 us  [both_sides(): lax.ppermute(block, 'row', [((row - turn) % rows, row) for row in range(r...]
    pallas_call x6 -> x9, Pallas kernels: 8.43 us -> 12.7 us  [the longest x4 6.37 us: with_writes(): pl.pallas_call(functools.partial(kernel, places), in_specs=specs, out_spe...]
    unnamed x14, local copies, waits for them, and re-layouts: 1.25 us -> 1.93 us
  transfers between devices with their start and end apart: 8 -> 16, of which waited for: 7 -> 3; matrix products, arithmetic and copies ran while one was open for 0% -> 0% of each run, Pallas kernels for 16% -> 25%
where the time goes in v1:
time: 53.7 us; the launch traced here: 53.4 us
  starting transfers between devices  31.9 us (59%)
  Pallas kernels  15 us (28%)
  local copies, waits for them, and re-layouts  2.9 us (5%)
  waiting for transfers between devices  2.81 us (5%)
  between operations  0.86 us (2%)
    ppermute x16, starting transfers between devices, both_sides(): lax.ppermute(block, 'row', [((row - turn) % rows, row) for row in range(r...  31.9 us
    pallas_call x4, Pallas kernels, with_writes(): pl.pallas_call(functools.partial(kernel, places), in_specs=specs, out_spe...  6.37 us
    pallas_call x4, Pallas kernels, mid_part(): pl.pallas_call(functools.partial(mid_kernel, span[0]), in_specs=[SMEM] +...  4.71 us
    ppermute x16, waiting for transfers between devices, both_sides(): lax.ppermute(block, 'row', [((row - turn) % rows, row) for row in range(r...  2.81 us
    pallas_call x1, Pallas kernels, banded(): pl.pallas_call(band_kernel, in_specs=[SMEM, VMEM], out_specs=VMEM, out_sh...  2.17 us
    unnamed x14, local copies, waits for them, and re-layouts  1.93 us
    pallas_call x1, Pallas kernels, last_part(): pl.pallas_call(functools.partial(last_kernel, span[0]), in_specs=[SMEM] *...  1.64 us
  transfers between devices with their start and end apart: 16, of which 3 were waited for; matrix products, arithmetic and copies ran while one was open for 0% of the time, Pallas kernels for 25%

profile of v1, /device:TPU:0, one launch (start us, length us, event | category | flops | bytes accessed | tf_op | source)
XLA Modules:
  0.0 53.4 jit_solution(6093323427933613574)
XLA Ops:
  0.6 1.0 %slice.7.here_ref = bf16[512,128]{1,0:T(8,128)(2,1)S(1)} slice(f32[512,512]{1,0:T(8,128)} %refs_3_), slice={[0:512], [0:128]} | slice | bytes 262144 | tf_op jit(solution)/shard_map/slice | solution.py:264
  1.6 3.1 %collective-permute-start = (bf16[512,128]{1,0:T(8,128)(2,1)S(1)}, bf16[512,128]{1,0:T(8,128)(2,1)S(1)}, u32[]{:S(2)}, u32[]{:S(2)}) collective-permute-start(bf16[512,128]{1,0:T(8,128)(2,1)S(1)} %slice.7.here_ref), channel_id=1, source_target_pairs={{12,0},{0,4},{4,8},{8,12},{13,1},{1,5},{5,9},{9,13},{14,2},{2,6},{... | collective-permute-start | bytes 393224 | tf_op jit(solution)/shard_map/ppermute | solution.py:28
  4.7 2.1 %collective-permute-start.1 = (bf16[512,128]{1,0:T(8,128)(2,1)S(1)}, bf16[512,128]{1,0:T(8,128)(2,1)S(1)}, u32[]{:S(2)}, u32[]{:S(2)}) collective-permute-start(bf16[512,128]{1,0:T(8,128)(2,1)S(1)} %slice.7.here_ref), channel_id=1, source_target_pairs={{4,0},{8,4},{12,8},{0,12},{5,1},{9,5},{13,9},{1,13},{6,2},{10,6},{... | collective-permute-start | bytes 393224 | tf_op jit(solution)/shard_map/ppermute | solution.py:28
  6.8 0.0 copy-start
  6.8 1.2 %copy-done = f32[512,512]{1,0:T(8,128)S(1)} copy-done((f32[512,512]{1,0:T(8,128)S(1)}, f32[512,512]{1,0:T(8,128)}, u32[]{:S(2)}) %copy-start) | copy-done | bytes 1048600
  8.0 0.0 copy-start.3
  8.0 0.1 round_part.1
  8.1 0.0 copy-start.2
  8.1 0.0 copy-start.4
  8.1 0.1 collective-permute-start.4
  8.2 3.8 %collective-permute-start.5 = (bf16[512,128]{1,0:T(8,128)(2,1)S(1)}, bf16[512,128]{1,0:T(8,128)(2,1)S(1)}, u32[]{:S(2)}, u32[]{:S(2)}) collective-permute-start(bf16[512,128]{1,0:T(8,128)(2,1)S(1)} %get-tuple-element.38.here_ref), channel_id=1, source_target_pairs={{4,0},{8,4},{12,8},{0,12},{5,1},{9,5},{13,9},{1,13},{6,2},{10,6},{... | collective-permute-start | bytes 393224 | tf_op jit(solution)/shard_map/ppermute | solution.py:28
  12.0 0.0 collective-permute-start.6
  12.0 0.0 collective-permute-done.first_ref
  12.0 3.8 %collective-permute-start.7 = (bf16[512,128]{1,0:T(8,128)(2,1)S(1)}, bf16[512,128]{1,0:T(8,128)(2,1)S(1)}, u32[]{:S(2)}, u32[]{:S(2)}) collective-permute-start(bf16[512,128]{1,0:T(8,128)(2,1)S(1)} %get-tuple-element.40.here_ref), channel_id=1, source_target_pairs={{4,0},{8,4},{12,8},{0,12},{5,1},{9,5},{13,9},{1,13},{6,2},{10,6},{... | collective-permute-start | bytes 393224 | tf_op jit(solution)/shard_map/ppermute | solution.py:28
  15.8 0.0 copy-done.3
  15.8 0.0 copy-start.6
  15.8 0.7 %copy-done.6 = s32[8,16]{1,0:T(8,128)S(1)} copy-done((s32[8,16]{1,0:T(8,128)S(1)}, s32[8,16]{1,0:T(8,128)}, u32[]{:S(2)}) %copy-start.6) | copy-done | bytes 536
  16.5 2.2 %band.1.band_ref.refs_2_.refs_0_ = bf16[512,1536]{1,0:T(8,128)(2,1)S(1)} custom-call(s32[8,16]{1,0:T(8,128)S(1)} %copy-done.6, bf16[8,64,1024]{2,1,0:T(8,128)(2,1)S(1)} %copy-done.3), custom_call_target="tpu_custom_call" | custom-call | flops 6291456 | bytes 2621440 | tf_op jit(solution)/shard_map/band/pallas_call | solution.py:85
  18.7 0.0 collective-permute-done.1.second_ref
  18.7 0.1 collective-permute-start.8
  18.7 0.0 copy-done.2
  18.7 0.0 copy-done.4
  18.8 1.2 %mid_part.4 = (f32[512,128]{1,0:T(8,128)S(1)}, bf16[512,128]{1,0:T(8,128)(2,1)S(1)}) custom-call(s32[8,8]{1,0:T(8,128)S(1)} %copy-done.4, bf16[512,1536]{1,0:T(8,128)(2,1)S(1)} %band.1.band_ref.refs_2_.refs_0_, bf16[512,128]{1,0:T(8,128)(2,1)S(1)} %slice.7.here_ref, bf16[512,128]{1,0:T(8,128)(2,1)S(1)} %collective-permute-done.first_ref, ...), custom_call_target="tpu_custom_call" | custom-call | flops 201326592 | bytes 2621440 | tf_op jit(solution)/shard_map/mid_part/pallas_call | solution.py:141
  19.9 0.0 collective-permute-done.4.first_ref
  19.9 3.8 %collective-permute-start.9 = (bf16[512,128]{1,0:T(8,128)(2,1)S(1)}, bf16[512,128]{1,0:T(8,128)(2,1)S(1)}, u32[]{:S(2)}, u32[]{:S(2)}) collective-permute-start(bf16[512,128]{1,0:T(8,128)(2,1)S(1)} %get-tuple-element.42.here_ref), channel_id=1, source_target_pairs={{4,0},{8,4},{12,8},{0,12},{5,1},{9,5},{13,9},{1,13},{6,2},{10,6},{... | collective-permute-start | bytes 393224 | tf_op jit(solution)/shard_map/ppermute | solution.py:28
  23.8 0.0 collective-permute-done.5.second_ref
  23.8 0.0 collective-permute-start.2
  23.8 0.0 collective-permute-done.6.first_ref
  23.8 3.8 %collective-permute-start.3 = (bf16[512,128]{1,0:T(8,128)(2,1)S(1)}, bf16[512,128]{1,0:T(8,128)(2,1)S(1)}, u32[]{:S(2)}, u32[]{:S(2)}) collective-permute-start(bf16[512,128]{1,0:T(8,128)(2,1)S(1)} %get-tuple-element.35.refs_3_), channel_id=1, source_target_pairs={{4,0},{8,4},{12,8},{0,12},{5,1},{9,5},{13,9},{1,13},{6,2},{10,6},{... | collective-permute-start | bytes 393224 | tf_op jit(solution)/shard_map/ppermute | solution.py:28
  27.6 1.2 %mid_part.5 = (f32[512,128]{1,0:T(8,128)S(1)}, bf16[512,128]{1,0:T(8,128)(2,1)S(1)}) custom-call(s32[8,8]{1,0:T(8,128)S(1)} %copy-done.4, bf16[512,1536]{1,0:T(8,128)(2,1)S(1)} %band.1.band_ref.refs_2_.refs_0_, bf16[512,128]{1,0:T(8,128)(2,1)S(1)} %get-tuple-element.38.here_ref, bf16[512,128]{1,0:T(8,128)(2,1)S(1)} %collective-permute-done.4.first_ref, ...), custom_call_target="tpu_custom_call" | custom-call | flops 201326592 | bytes 2621440 | tf_op jit(solution)/shard_map/mid_part/pallas_call | solution.py:141
  28.8 0.0 collective-permute-done.7.second_ref
  28.8 0.1 collective-permute-start.14
  28.9 0.0 collective-permute-done.8.first_ref
  28.9 3.8 %collective-permute-start.15 = (bf16[512,128]{1,0:T(8,128)(2,1)S(1)}, bf16[512,128]{1,0:T(8,128)(2,1)S(1)}, u32[]{:S(2)}, u32[]{:S(2)}) collective-permute-start(bf16[512,128]{1,0:T(8,128)(2,1)S(1)} %get-tuple-element.47.refs_3_), channel_id=1, source_target_pairs={{4,0},{8,4},{12,8},{0,12},{5,1},{9,5},{13,9},{1,13},{6,2},{10,6},{... | collective-permute-start | bytes 393224 | tf_op jit(solution)/shard_map/ppermute | solution.py:28
  32.7 1.2 %mid_part.6 = (f32[512,128]{1,0:T(8,128)S(1)}, bf16[512,128]{1,0:T(8,128)(2,1)S(1)}) custom-call(s32[8,8]{1,0:T(8,128)S(1)} %copy-done.4, bf16[512,1536]{1,0:T(8,128)(2,1)S(1)} %band.1.band_ref.refs_2_.refs_0_, bf16[512,128]{1,0:T(8,128)(2,1)S(1)} %get-tuple-element.40.here_ref, bf16[512,128]{1,0:T(8,128)(2,1)S(1)} %collective-permute-done.6.first_ref, ...), custom_call_target="tpu_custom_call" | custom-call | flops 201326592 | bytes 2621440 | tf_op jit(solution)/shard_map/mid_part/pallas_call | solution.py:141
  33.9 0.0 collective-permute-done.9.second_ref
  33.9 0.1 collective-permute-start.12
  34.0 0.0 collective-permute-done.2.refs_4_
  34.0 3.8 %collective-permute-start.13 = (bf16[512,128]{1,0:T(8,128)(2,1)S(1)}, bf16[512,128]{1,0:T(8,128)(2,1)S(1)}, u32[]{:S(2)}, u32[]{:S(2)}) collective-permute-start(bf16[512,128]{1,0:T(8,128)(2,1)S(1)} %get-tuple-element.46.refs_3_), channel_id=1, source_target_pairs={{4,0},{8,4},{12,8},{0,12},{5,1},{9,5},{13,9},{1,13},{6,2},{10,6},{... | collective-permute-start | bytes 393224 | tf_op jit(solution)/shard_map/ppermute | solution.py:28
  37.8 0.0 copy-start.1
  37.8 0.0 copy-start.5
  37.8 1.2 %mid_part.7 = (f32[512,128]{1,0:T(8,128)S(1)}, bf16[512,128]{1,0:T(8,128)(2,1)S(1)}) custom-call(s32[8,8]{1,0:T(8,128)S(1)} %copy-done.4, bf16[512,1536]{1,0:T(8,128)(2,1)S(1)} %band.1.band_ref.refs_2_.refs_0_, bf16[512,128]{1,0:T(8,128)(2,1)S(1)} %get-tuple-element.42.here_ref, bf16[512,128]{1,0:T(8,128)(2,1)S(1)} %collective-permute-done.8.first_ref, ...), custom_call_target="tpu_custom_call" | custom-call | flops 201326592 | bytes 2621440 | tf_op jit(solution)/shard_map/mid_part/pallas_call | solution.py:141
  39.0 0.0 collective-permute-done.3.refs_5_
  39.0 0.1 collective-permute-start.11
  39.0 0.3 collective-permute-done.14.refs_4_
  39.3 3.5 %collective-permute-start.10 = (bf16[512,128]{1,0:T(8,128)(2,1)S(1)}, bf16[512,128]{1,0:T(8,128)(2,1)S(1)}, u32[]{:S(2)}, u32[]{:S(2)}) collective-permute-start(bf16[512,128]{1,0:T(8,128)(2,1)S(1)} %get-tuple-element.45.refs_1_), channel_id=1, source_target_pairs={{4,0},{8,4},{12,8},{0,12},{5,1},{9,5},{13,9},{1,13},{6,2},{10,6},{... | collective-permute-start | bytes 393224 | tf_op jit(solution)/shard_map/ppermute | solution.py:28
  42.9 0.0 copy-done.1
  42.9 0.0 copy-done.5
  42.9 2.0 %next_part.3 = (f32[512,128]{1,0:T(8,128)S(1)}, f32[512,128]{1,0:T(8,128)S(1)}, f32[512,512]{1,0:T(8,128)}) custom-call(s32[8,8]{1,0:T(8,128)S(1)} %copy-done.4, f32[2]{0:T(128)S(1)} %copy-done.5, bf16[512,1536]{1,0:T(8,128)(2,1)S(1)} %band.1.band_ref.refs_2_.refs_0_, bf16[512,128]{1,0:T(8,128)(2,1)S(1)} %get-tuple-element.35.refs_3_, ...), custom_call_target="tpu_custom_call" | custom-call | flops 201326592 | bytes 2055208 | tf_op jit(solution)/shard_map/next_part/pallas_call | solution.py:187
  44.9 0.0 collective-permute-done.15.refs_5_
  44.9 1.2 %next_part.4 = (f32[512,128]{1,0:T(8,128)S(1)}, f32[512,128]{1,0:T(8,128)S(1)}) custom-call(s32[8,8]{1,0:T(8,128)S(1)} %copy-done.4, f32[2]{0:T(128)S(1)} %copy-done.5, bf16[512,1536]{1,0:T(8,128)(2,1)S(1)} %band.1.band_ref.refs_2_.refs_0_, bf16[512,128]{1,0:T(8,128)(2,1)S(1)} %get-tuple-element.47.refs_3_, ...), custom_call_target="tpu_custom_call" | custom-call | flops 201326592 | bytes 1006632 | tf_op jit(solution)/shard_map/next_part/pallas_call | solution.py:187
  46.1 0.0 collective-permute-done.12.refs_4_
  46.1 1.5 %collective-permute-done.13.refs_5_ = bf16[512,128]{1,0:T(8,128)(2,1)S(1)} collective-permute-done((bf16[512,128]{1,0:T(8,128)(2,1)S(1)}, bf16[512,128]{1,0:T(8,128)(2,1)S(1)}, u32[]{:S(2)}, u32[]{:S(2)}) %collective-permute-start.13) | collective-permute-done | bytes 131104 | tf_op jit(solution)/shard_map/ppermute | solution.py:28
  47.6 2.1 %next_part.5 = (f32[512,128]{1,0:T(8,128)S(1)}, f32[512,128]{1,0:T(8,128)S(1)}, f32[512,512]{1,0:T(8,128)}, f32[512,512]{1,0:T(8,128)}) custom-call(s32[8,8]{1,0:T(8,128)S(1)} %copy-done.4, f32[2]{0:T(128)S(1)} %copy-done.5, bf16[512,1536]{1,0:T(8,128)(2,1)S(1)} %band.1.band_ref.refs_2_.refs_0_, bf16[512,128]{1,0:T(8,128)(2,1)S(1)} %get-tuple-element.46.refs_3_, ...), custom_call_target="tpu_custom_call" | custom-call | flops 201326592 | bytes 2055208 | tf_op jit(solution)/shard_map/next_part/pallas_call | solution.py:187
  49.7 1.0 %collective-permute-done.11.refs_2_ = bf16[512,128]{1,0:T(8,128)(2,1)S(1)} collective-permute-done((bf16[512,128]{1,0:T(8,128)(2,1)S(1)}, bf16[512,128]{1,0:T(8,128)(2,1)S(1)}, u32[]{:S(2)}, u32[]{:S(2)}) %collective-permute-start.11) | collective-permute-done | bytes 131104 | tf_op jit(solution)/shard_map/ppermute | solution.py:28
  50.7 1.1 %begun_part.1 = (f32[512,128]{1,0:T(8,128)S(1)}, f32[512,512]{1,0:T(8,128)}, f32[512,512]{1,0:T(8,128)}) custom-call(bf16[512,1536]{1,0:T(8,128)(2,1)S(1)} %band.1.band_ref.refs_2_.refs_0_, bf16[512,128]{1,0:T(8,128)(2,1)S(1)} %get-tuple-element.45.refs_1_, ...), custom_call_target="tpu_custom_call", output_to_operand_aliasing={{1}: (6, {}), {2}: (7, {})} | custom-call | flops 134217728 | bytes 1195376 | tf_op jit(solution)/shard_map/begun_part/pallas_call | solution.py:187
  51.8 0.0 collective-permute-done.10.second_ref
  51.8 1.6 %last_part.1 = (f32[512,512]{1,0:T(8,128)}, f32[512,512]{1,0:T(8,128)}) custom-call(s32[8,8]{1,0:T(8,128)S(1)} %copy-done.4, f32[2]{0:T(128)S(1)} %copy-done.5, bf16[512,1536]{1,0:T(8,128)(2,1)S(1)} %band.1.band_ref.refs_2_.refs_0_, bf16[512,128]{1,0:T(8,128)(2,1)S(1)} %collective-permute-done.10.second_ref, ...), custom_call_target="tpu_custom_call", output_to_operand_aliasing={{0}: (6, {}), {1}: (7, {})} | custom-call | flops 67108864 | bytes 1966080 | tf_op jit(solution)/shard_map/last_part/pallas_call | solution.py:247
Async XLA Ops:
  1.6 10.4 %collective-permute-start = (bf16[512,128]{1,0:T(8,128)(2,1)S(1)}, bf16[512,128]{1,0:T(8,128)(2,1)S(1)}, u32[]{:S(2)}, u32[]{:S(2)}) collective-permute-start(bf16[512,128]{1,0:T(8,128)(2,1)S(1)} %slice.7.here_ref), channel_id=1, source_target_pairs={{12,0},{0,4},{4,8},{8,12},{13,1},{1,5},{5,9},{9,13},{14,2},{2,6},{... | collective-permute-start | bytes 393224 | tf_op jit(solution)/shard_map/ppermute | solution.py:28
  4.7 14.0 %collective-permute-start.1 = (bf16[512,128]{1,0:T(8,128)(2,1)S(1)}, bf16[512,128]{1,0:T(8,128)(2,1)S(1)}, u32[]{:S(2)}, u32[]{:S(2)}) collective-permute-start(bf16[512,128]{1,0:T(8,128)(2,1)S(1)} %slice.7.here_ref), channel_id=1, source_target_pairs={{4,0},{8,4},{12,8},{0,12},{5,1},{9,5},{13,9},{1,13},{6,2},{10,6},{... | collective-permute-start | bytes 393224 | tf_op jit(solution)/shard_map/ppermute | solution.py:28
  6.8 1.2 %copy-start = (f32[512,512]{1,0:T(8,128)S(1)}, f32[512,512]{1,0:T(8,128)}, u32[]{:S(2)}) copy-start(f32[512,512]{1,0:T(8,128)} %refs_3_) | copy-start | bytes 3145732
  8.0 7.8 %copy-start.3 = (bf16[8,64,1024]{2,1,0:T(8,128)(2,1)S(1)}, bf16[8,64,1024]{2,1,0:T(8,128)(2,1)}, u32[]{:S(2)}) copy-start(bf16[8,64,1024]{2,1,0:T(8,128)(2,1)} %strips_ref) | copy-start | bytes 3145732
  8.1 10.7 %copy-start.2 = (f32[512,512]{1,0:T(8,128)S(1)}, f32[512,512]{1,0:T(8,128)}, u32[]{:S(2)}) copy-start(f32[512,512]{1,0:T(8,128)} %prev_ref.3) | copy-start | bytes 3145732
  8.1 10.7 %copy-start.4 = (s32[8,8]{1,0:T(8,128)S(1)}, s32[8,8]{1,0:T(8,128)}, u32[]{:S(2)}) copy-start(s32[8,8]{1,0:T(8,128)} %mask_ref.9) | copy-start | bytes 772
  8.1 11.9 %collective-permute-start.4 = (bf16[512,128]{1,0:T(8,128)(2,1)S(1)}, bf16[512,128]{1,0:T(8,128)(2,1)S(1)}, u32[]{:S(2)}, u32[]{:S(2)}) collective-permute-start(bf16[512,128]{1,0:T(8,128)(2,1)S(1)} %get-tuple-element.38.here_ref), channel_id=1, source_target_pairs={{12,0},{0,4},{4,8},{8,12},{13,1},{1,5},{5,9},{9,13},{14,2},{2,6},{... | collective-permute-start | bytes 393224 | tf_op jit(solution)/shard_map/ppermute | solution.py:28
  8.2 15.6 %collective-permute-start.5 = (bf16[512,128]{1,0:T(8,128)(2,1)S(1)}, bf16[512,128]{1,0:T(8,128)(2,1)S(1)}, u32[]{:S(2)}, u32[]{:S(2)}) collective-permute-start(bf16[512,128]{1,0:T(8,128)(2,1)S(1)} %get-tuple-element.38.here_ref), channel_id=1, source_target_pairs={{4,0},{8,4},{12,8},{0,12},{5,1},{9,5},{13,9},{1,13},{6,2},{10,6},{... | collective-permute-start | bytes 393224 | tf_op jit(solution)/shard_map/ppermute | solution.py:28
  12.0 11.8 %collective-permute-start.6 = (bf16[512,128]{1,0:T(8,128)(2,1)S(1)}, bf16[512,128]{1,0:T(8,128)(2,1)S(1)}, u32[]{:S(2)}, u32[]{:S(2)}) collective-permute-start(bf16[512,128]{1,0:T(8,128)(2,1)S(1)} %get-tuple-element.40.here_ref), channel_id=1, source_target_pairs={{12,0},{0,4},{4,8},{8,12},{13,1},{1,5},{5,9},{9,13},{14,2},{2,6},{... | collective-permute-start | bytes 393224 | tf_op jit(solution)/shard_map/ppermute | solution.py:28
  12.0 16.8 %collective-permute-start.7 = (bf16[512,128]{1,0:T(8,128)(2,1)S(1)}, bf16[512,128]{1,0:T(8,128)(2,1)S(1)}, u32[]{:S(2)}, u32[]{:S(2)}) collective-permute-start(bf16[512,128]{1,0:T(8,128)(2,1)S(1)} %get-tuple-element.40.here_ref), channel_id=1, source_target_pairs={{4,0},{8,4},{12,8},{0,12},{5,1},{9,5},{13,9},{1,13},{6,2},{10,6},{... | collective-permute-start | bytes 393224 | tf_op jit(solution)/shard_map/ppermute | solution.py:28
  15.8 0.7 %copy-start.6 = (s32[8,16]{1,0:T(8,128)S(1)}, s32[8,16]{1,0:T(8,128)}, u32[]{:S(2)}) copy-start(s32[8,16]{1,0:T(8,128)} %slots_ref.1) | copy-start | bytes 1540
  18.7 10.2 %collective-permute-start.8 = (bf16[512,128]{1,0:T(8,128)(2,1)S(1)}, bf16[512,128]{1,0:T(8,128)(2,1)S(1)}, u32[]{:S(2)}, u32[]{:S(2)}) collective-permute-start(bf16[512,128]{1,0:T(8,128)(2,1)S(1)} %get-tuple-element.42.here_ref), channel_id=1, source_target_pairs={{12,0},{0,4},{4,8},{8,12},{13,1},{1,5},{5,9},{9,13},{14,2},{2,6},{... | collective-permute-start | bytes 393224 | tf_op jit(solution)/shard_map/ppermute | solution.py:28
  19.9 13.9 %collective-permute-start.9 = (bf16[512,128]{1,0:T(8,128)(2,1)S(1)}, bf16[512,128]{1,0:T(8,128)(2,1)S(1)}, u32[]{:S(2)}, u32[]{:S(2)}) collective-permute-start(bf16[512,128]{1,0:T(8,128)(2,1)S(1)} %get-tuple-element.42.here_ref), channel_id=1, source_target_pairs={{4,0},{8,4},{12,8},{0,12},{5,1},{9,5},{13,9},{1,13},{6,2},{10,6},{... | collective-permute-start | bytes 393224 | tf_op jit(solution)/shard_map/ppermute | solution.py:28
  23.8 10.2 %collective-permute-start.2 = (bf16[512,128]{1,0:T(8,128)(2,1)S(1)}, bf16[512,128]{1,0:T(8,128)(2,1)S(1)}, u32[]{:S(2)}, u32[]{:S(2)}) collective-permute-start(bf16[512,128]{1,0:T(8,128)(2,1)S(1)} %get-tuple-element.35.refs_3_), channel_id=1, source_target_pairs={{12,0},{0,4},{4,8},{8,12},{13,1},{1,5},{5,9},{9,13},{14,2},{2,6},{... | collective-permute-start | bytes 393224 | tf_op jit(solution)/shard_map/ppermute | solution.py:28
  23.8 15.2 %collective-permute-start.3 = (bf16[512,128]{1,0:T(8,128)(2,1)S(1)}, bf16[512,128]{1,0:T(8,128)(2,1)S(1)}, u32[]{:S(2)}, u32[]{:S(2)}) collective-permute-start(bf16[512,128]{1,0:T(8,128)(2,1)S(1)} %get-tuple-element.35.refs_3_), channel_id=1, source_target_pairs={{4,0},{8,4},{12,8},{0,12},{5,1},{9,5},{13,9},{1,13},{6,2},{10,6},{... | collective-permute-start | bytes 393224 | tf_op jit(solution)/shard_map/ppermute | solution.py:28
  28.8 10.5 %collective-permute-start.14 = (bf16[512,128]{1,0:T(8,128)(2,1)S(1)}, bf16[512,128]{1,0:T(8,128)(2,1)S(1)}, u32[]{:S(2)}, u32[]{:S(2)}) collective-permute-start(bf16[512,128]{1,0:T(8,128)(2,1)S(1)} %get-tuple-element.47.refs_3_), channel_id=1, source_target_pairs={{12,0},{0,4},{4,8},{8,12},{13,1},{1,5},{5,9},{9,13},{14,2},{2,6},{... | collective-permute-start | bytes 393224 | tf_op jit(solution)/shard_map/ppermute | solution.py:28
  28.9 16.0 %collective-permute-start.15 = (bf16[512,128]{1,0:T(8,128)(2,1)S(1)}, bf16[512,128]{1,0:T(8,128)(2,1)S(1)}, u32[]{:S(2)}, u32[]{:S(2)}) collective-permute-start(bf16[512,128]{1,0:T(8,128)(2,1)S(1)} %get-tuple-element.47.refs_3_), channel_id=1, source_target_pairs={{4,0},{8,4},{12,8},{0,12},{5,1},{9,5},{13,9},{1,13},{6,2},{10,6},{... | collective-permute-start | bytes 393224 | tf_op jit(solution)/shard_map/ppermute | solution.py:28
  33.9 12.2 %collective-permute-start.12 = (bf16[512,128]{1,0:T(8,128)(2,1)S(1)}, bf16[512,128]{1,0:T(8,128)(2,1)S(1)}, u32[]{:S(2)}, u32[]{:S(2)}) collective-permute-start(bf16[512,128]{1,0:T(8,128)(2,1)S(1)} %get-tuple-element.46.refs_3_), channel_id=1, source_target_pairs={{12,0},{0,4},{4,8},{8,12},{13,1},{1,5},{5,9},{9,13},{14,2},{2,6},{... | collective-permute-start | bytes 393224 | tf_op jit(solution)/shard_map/ppermute | solution.py:28
  34.0 13.6 %collective-permute-start.13 = (bf16[512,128]{1,0:T(8,128)(2,1)S(1)}, bf16[512,128]{1,0:T(8,128)(2,1)S(1)}, u32[]{:S(2)}, u32[]{:S(2)}) collective-permute-start(bf16[512,128]{1,0:T(8,128)(2,1)S(1)} %get-tuple-element.46.refs_3_), channel_id=1, source_target_pairs={{4,0},{8,4},{12,8},{0,12},{5,1},{9,5},{13,9},{1,13},{6,2},{10,6},{... | collective-permute-start | bytes 393224 | tf_op jit(solution)/shard_map/ppermute | solution.py:28
  37.8 5.1 %copy-start.1 = (f32[512,512]{1,0:T(8,128)S(1)}, f32[512,512]{1,0:T(8,128)}, u32[]{:S(2)}) copy-start(f32[512,512]{1,0:T(8,128)} %refs_3_) | copy-start | bytes 3145732
  37.8 5.1 %copy-start.5 = (f32[2]{0:T(128)S(1)}, f32[2]{0:T(128)}, u32[]{:S(2)}) copy-start(f32[2]{0:T(128)} %coeffs_ref.1) | copy-start | bytes 28
  39.0 11.7 %collective-permute-start.11 = (bf16[512,128]{1,0:T(8,128)(2,1)S(1)}, bf16[512,128]{1,0:T(8,128)(2,1)S(1)}, u32[]{:S(2)}, u32[]{:S(2)}) collective-permute-start(bf16[512,128]{1,0:T(8,128)(2,1)S(1)} %get-tuple-element.45.refs_1_), channel_id=1, source_target_pairs={{12,0},{0,4},{4,8},{8,12},{13,1},{1,5},{5,9},{9,13},{14,2},{2,6},{... | collective-permute-start | bytes 393224 | tf_op jit(solution)/shard_map/ppermute | solution.py:28
  39.3 12.5 %collective-permute-start.10 = (bf16[512,128]{1,0:T(8,128)(2,1)S(1)}, bf16[512,128]{1,0:T(8,128)(2,1)S(1)}, u32[]{:S(2)}, u32[]{:S(2)}) collective-permute-start(bf16[512,128]{1,0:T(8,128)(2,1)S(1)} %get-tuple-element.45.refs_1_), channel_id=1, source_target_pairs={{4,0},{8,4},{12,8},{0,12},{5,1},{9,5},{13,9},{1,13},{6,2},{10,6},{... | collective-permute-start | bytes 393224 | tf_op jit(solution)/shard_map/ppermute | solution.py:28

commit v2 on v1

--- a/solution.py
+++ b/solution.py
@@ -18,14 +18,18 @@
 
 
 def spans_of(columns):
-    width = columns // 4 if columns % (4 * LANES) == 0 else LANES
-    return [(start, width) for start in range(0, columns, width)]
+    if columns % (4 * LANES):
+        ones = [(start, LANES) for start in range(0, columns, LANES)]
+        return ones, ones
+    half, quarter = columns // 2, columns // 4
+    return [(0, half), (half, half)], [(0, half), (half, quarter), (half + quarter, quarter)]
 
 
 def both_sides(block):
     rows = lax.axis_size("row")
-    return tuple(
-        lax.ppermute(block, "row", [((row - turn) % rows, row) for row in range(rows)]) for turn in (1, -1))
+    second = lax.ppermute(block, "row", [((row + 1) % rows, row) for row in range(rows)])
+    first = lax.ppermute(block, "row", [((row - 1) % rows, row) for row in range(rows)])
+    return first, second
 
 
 def side_columns(depth, order):
@@ -127,29 +131,34 @@
     return copies
 
 
-def mid_kernel(start, mask_ref, band_ref, here_ref, first_ref, second_ref, prev_ref, *rest):
-    mid_ref, round_ref = rest[-2:]
+def mid_kernel(start, pieces, mask_ref, band_ref, here_ref, second_ref, first_ref, prev_ref, *rest):
+    mid_ref, round_refs = rest[-pieces - 1], rest[-pieces:]
     total = product(band_ref, here_ref, first_ref, second_ref)
     term = 2.0 * total - prev_ref[:, start:start + here_ref.shape[1]]
     for at, value in masked(start, mask_ref, term):
         mid_ref[at, :] = value
-        round_ref[at, :] = value.astype(jnp.bfloat16)
-
-
-def mid_part(span, mask, band, here, first, second, prev, after):
+        from_column = 0
+        for round_ref in round_refs:
+            to_column = from_column + round_ref.shape[1]
+            round_ref[at, :] = value[:, from_column:to_column].astype(jnp.bfloat16)
+            from_column = to_column
+
+
+def mid_part(span, widths, mask, band, here, first, second, prev, after):
     rows, width = here.shape
     return pl.pallas_call(
-        functools.partial(mid_kernel, span[0]),
+        functools.partial(mid_kernel, span[0], len(widths)),
         in_specs=[SMEM] + [VMEM] * 5 + [ANY] * len(after),
-        out_specs=[VMEM] * 2,
-        out_shape=[jax.ShapeDtypeStruct(here.shape, jnp.float32), jax.ShapeDtypeStruct(here.shape, jnp.bfloat16)],
+        out_specs=[VMEM] * (1 + len(widths)),
+        out_shape=[jax.ShapeDtypeStruct(here.shape, jnp.float32)]
+        + [jax.ShapeDtypeStruct((rows, piece), jnp.bfloat16) for piece in widths],
         compiler_params=params(),
         cost_estimate=cost(6 * rows * rows * width, 6 * rows * rows + 16 * rows * width),
         name="mid_part",
-    )(mask, band, here, first, second, prev, *after)
-
-
-def next_kernel(start, places, panels, unread, mask_ref, coeffs_ref, band_ref, here_ref, first_ref, second_ref, now_ref,
+    )(mask, band, here, second, first, prev, *after)
+
+
+def next_kernel(start, mid_start, places, panels, unread, mask_ref, coeffs_ref, band_ref, here_ref, second_ref, first_ref, now_ref,
                 mid_ref, *rest):
     rest = rest[unread:]
     held_refs, rest = rest[:len(places)], rest[len(places):]
@@ -160,19 +169,15 @@
     term = 2.0 * total - now_ref[:, start:start + here_ref.shape[1]]
     for at, value in masked(start, mask_ref, term):
         next_ref[at, :] = value
-        density_ref[at, :] = coeffs_ref[0] * mid_ref[at, :] + coeffs_ref[1] * value
+        mid = mid_ref[at, mid_start:mid_start + here_ref.shape[1]]
+        density_ref[at, :] = coeffs_ref[0] * mid + coeffs_ref[1] * value
     for copy in copies:
         copy.wait()
 
 
-def begun_kernel(start, places, panels, band_ref, here_ref, first_ref, now_ref, *rest):
-    held_refs, rest = rest[:len(places)], rest[len(places):]
-    sums_ref, sems = rest[-panels - 2], rest[-1]
-    out_refs = rest[-panels - 1:-1]
-    copies = writes([(held, out_refs[o], at) for held, (o, at) in zip(held_refs, places)], sems)
+def begun_kernel(start, band_ref, here_ref, first_ref, now_ref, *rest):
+    sums_ref = rest[-1]
     sums_ref[...] = 2.0 * product(band_ref, here_ref, first_ref) - now_ref[:, start:start + here_ref.shape[1]]
-    for copy in copies:
-        copy.wait()
 
 
 def with_writes(kernel, specs, operands, out_shapes, moves, panels, whole, outs, flops, name):
@@ -198,31 +203,36 @@
     return results[:len(out_shapes)], tuple(results[len(out_shapes):])
 
 
-def next_part(span, mask, coeffs, band, here, first, second, now, mid, after, moves, panels):
+def next_part(span, mid_start, mask, coeffs, band, here, first, second, now, mid, after, moves, panels):
     rows, width = here.shape
     return with_writes(
-        lambda places, *refs: next_kernel(span[0], places, panels, len(after), *refs),
-        [SMEM] * 2 + [VMEM] * 6 + [ANY] * len(after), [mask, coeffs, band, here, first, second, now, mid, *after],
+        lambda places, *refs: next_kernel(span[0], mid_start, places, panels, len(after), *refs),
+        [SMEM] * 2 + [VMEM] * 6 + [ANY] * len(after), [mask, coeffs, band, here, second, first, now, mid, *after],
         [jax.ShapeDtypeStruct(here.shape, jnp.float32)] * 2, moves, panels, now.shape, None,
         6 * rows * rows * width, "next_part")
 
 
-def begun_part(span, band, here, first, now, moves, panels, outs):
+def begun_part(span, band, here, first, now, after):
     rows, width = here.shape
-    (sums,), outs = with_writes(
-        lambda places, *refs: begun_kernel(span[0], places, panels, *refs),
-        [VMEM] * 4, [band, here, first, now],
-        [jax.ShapeDtypeStruct(here.shape, jnp.float32)], moves, panels, now.shape, outs,
-        4 * rows * rows * width, "begun_part")
-    return sums, outs
-
-
-def last_kernel(start, mask_ref, coeffs_ref, band_ref, second_ref, sums_ref, mid_ref, *rest):
-    next_ref, density_ref, held_next, held_density, sems = rest[-5:]
+    return pl.pallas_call(
+        functools.partial(begun_kernel, span[0]),
+        in_specs=[VMEM] * 4 + [ANY] * len(after),
+        out_specs=VMEM,
+        out_shape=jax.ShapeDtypeStruct(here.shape, jnp.float32),
+        compiler_params=params(),
+        cost_estimate=cost(4 * rows * rows * width, 4 * rows * rows + 12 * rows * width),
+        name="begun_part",
+    )(band, here, first, now, *after)
+
+
+def last_kernel(start, mid_start, places, mask_ref, coeffs_ref, band_ref, second_ref, sums_ref, mid_ref, *rest):
+    held_refs = rest[:len(places)]
+    next_ref, density_ref, held_next, held_density, early_sems, sems = rest[-6:]
+    copies = writes([(held, (next_ref, density_ref)[o], at) for held, (o, at) in zip(held_refs, places)], early_sems)
+    early = len(copies)
     rows, width = second_ref.shape
     block = rows // mask_ref.shape[0]
     step = rows // CHUNKS
-    copies = []
     for c in range(CHUNKS):
         total = jnp.dot(
             band_ref[c * step:(c + 1) * step, side_columns(rows, 1)], second_ref[...],
@@ -232,65 +242,73 @@
             keep = kept(mask_ref, c * (step // block) + i, start // block, block, width)
             value = jnp.where(keep, 2.0 * total[i * block:(i + 1) * block] + sums_ref[at, :], 0.0)
             held_next[at, :] = value
-            held_density[at, :] = coeffs_ref[0] * mid_ref[at, :] + coeffs_ref[1] * value
+            density = coeffs_ref[0] * mid_ref[at, mid_start:mid_start + width] + coeffs_ref[1] * value
+            held_density[at, :] = density
         done = pl.ds(c * step, step)
         for held, out_ref in ((held_next, next_ref), (held_density, density_ref)):
             copies.append(pltpu.make_async_copy(
-                held.at[done, :], out_ref.at[done, pl.ds(start, width)], sems.at[len(copies)]))
+                held.at[done, :], out_ref.at[done, pl.ds(start, width)], sems.at[len(copies) - early]))
             copies[-1].start()
     for copy in copies:
         copy.wait()
 
 
-def last_part(span, mask, coeffs, band, second, sums, mid, outs):
+def last_part(span, mid_start, mask, coeffs, band, second, sums, mid, moves, outs):
     rows, width = second.shape
+    held = [part for part, _ in moves]
     return pl.pallas_call(
-        functools.partial(last_kernel, span[0]),
-        in_specs=[SMEM] * 2 + [VMEM] * 4 + [HBM] * 2,
+        functools.partial(last_kernel, span[0], mid_start, [place for _, place in moves]),
+        in_specs=[SMEM] * 2 + [VMEM] * (4 + len(held)) + [HBM] * 2,
         out_specs=[HBM] * 2,
         out_shape=[jax.ShapeDtypeStruct(out.shape, jnp.float32) for out in outs],
-        scratch_shapes=[pltpu.VMEM((rows, width), jnp.float32)] * 2 + [pltpu.SemaphoreType.DMA((2 * CHUNKS,))],
-        input_output_aliases={6: 0, 7: 1},
+        scratch_shapes=[pltpu.VMEM((rows, width), jnp.float32)] * 2
+        + [pltpu.SemaphoreType.DMA((max(len(held), 1),)), pltpu.SemaphoreType.DMA((2 * CHUNKS,))],
+        input_output_aliases={6 + len(held): 0, 7 + len(held): 1},
         compiler_params=params(),
         cost_estimate=cost(2 * rows * rows * width, 2 * rows * rows + 22 * rows * width),
         name="last_part",
-    )(mask, coeffs, band, second, sums, mid, *outs)
+    )(mask, coeffs, band, second, sums, mid, *held, *outs)
 
 
 def local(h_strips, h_slots, t_prev, t_now, t_mask, coeffs):
-    spans = spans_of(t_now.shape[1])
-    parts = len(spans)
+    spans, spans_next = spans_of(t_now.shape[1])
     start, width = spans[0]
     here = [t_now[:, start:start + width].astype(jnp.bfloat16)]
     here[0], t_now, t_prev, h_strips = lax.optimization_barrier((here[0], t_now, t_prev, h_strips))
     here += rounded(t_now, spans[1:])
     band = banded(h_slots, h_strips)
     sides = [both_sides(block) for block in here]
-    mids, here_mid, sides_mid = [], [], []
-    for part in range(parts):
-        first, second = sides[part]
-        mid, low = mid_part(spans[part], t_mask, band, here[part], first, second, t_prev, mids[-1:])
+    mids, here_mid, sides_mid, origin = [], [], [], []
+    for part, (start, width) in enumerate(spans):
+        inside = [span for span in spans_next if start <= span[0] < start + width]
+        mid, *lows = mid_part(
+            spans[part], [piece for _, piece in inside], t_mask, band, here[part], *sides[part], t_prev, mids[-1:])
         mids.append(mid)
-        here_mid.append(low)
-        sides_mid.append(both_sides(low))
+        here_mid += lows
+        sides_mid += [both_sides(low) for low in lows]
+        origin += [(part, span[0] - start) for span in inside]
     t_mid, outs, waiting, after = None, None, [], []
-    for part in range(parts - 1):
+    last = len(spans_next) - 1
+    for part, span in enumerate(spans_next[:-1]):
         panels, moves = 0, []
         if part == 0:
-            panels, moves = 1, [(mids[p], (0, spans[p][0])) for p in range(parts)]
-        elif part == parts - 2:
-            panels, moves = 2, waiting
+            panels, moves = 1, [(mid, (0, spans[p][0])) for p, mid in enumerate(mids)]
+        elif part == last - 1:
+            panels, moves, waiting = 2, waiting, []
+        source, mid_start = origin[part]
         (term, density), written = next_part(
-            spans[part], t_mask, coeffs, band, here_mid[part], *sides_mid[part], t_now, mids[part], after, moves, panels)
+            span, mid_start, t_mask, coeffs, band, here_mid[part], *sides_mid[part], t_now, mids[source], after,
+            moves, panels)
         after = [term]
         if part == 0:
             t_mid = written[0]
-        elif part == parts - 2:
-            outs, waiting = written, []
-        waiting += [(term, (0, spans[part][0])), (density, (1, spans[part][0]))]
-    first, second = sides_mid[-1]
-    sums, outs = begun_part(spans[-1], band, here_mid[-1], first, t_now, waiting, 2, outs)
-    outs = last_part(spans[-1], t_mask, coeffs, band, second, sums, mids[-1], outs)
+        elif part == last - 1:
+            outs = written
+        waiting = waiting + [(term, (0, span[0])), (density, (1, span[0]))]
+    first, second = sides_mid[last]
+    source, mid_start = origin[last]
+    sums = begun_part(spans_next[last], band, here_mid[last], first, t_now, after)
+    outs = last_part(spans_next[last], mid_start, t_mask, coeffs, band, second, sums, mids[source], waiting, outs)
     return (t_mid, outs[0], outs[1])
 
 

time: 53.7 us -> 53.7 us (level)
  waiting for transfers between devices: 2.81 us -> 15.3 us
  starting transfers between devices: 31.9 us -> 24.3 us
  Pallas kernels: 15 us -> 10.8 us
  local copies, waits for them, and re-layouts: 2.9 us -> 2.33 us
    ppermute x16 -> x10, waiting for transfers between devices: 2.81 us -> 15.3 us  [the longest x5 13.5 us: both_sides(): lax.ppermute(block, 'row', [((row + 1) % rows, row) for row in range(rows)])]
    ppermute x16 -> x10, starting transfers between devices: 31.9 us -> 24.3 us  [the longest x5 20.1 us: both_sides(): lax.ppermute(block, 'row', [((row + 1) % rows, row) for row in range(rows)])]
    pallas_call x4 -> x2, Pallas kernels: 6.37 us -> 4.19 us  [with_writes(): pl.pallas_call(functools.partial(kernel, places), in_specs=specs, out_spe...]
    pallas_call x5 -> x4, Pallas kernels: 6.35 us -> 4.45 us  [the longest x2 2.35 us: mid_part(): pl.pallas_call(functools.partial(mid_kernel, span[0], len(widths)), in_sp...]
    unnamed x14, local copies, waits for them, and re-layouts: 1.93 us -> 1.25 us
  transfers between devices with their start and end apart: 16 -> 10, of which waited for: 3 -> 7; matrix products, arithmetic and copies ran while one was open for 0% -> 0% of each run, Pallas kernels for 25% -> 17%
where the time goes in v2:
time: 53.7 us; the launch traced here: 53.5 us
  starting transfers between devices  24.3 us (45%)
  waiting for transfers between devices  15.3 us (28%)
  Pallas kernels  10.8 us (20%)
  local copies, waits for them, and re-layouts  2.33 us (4%)
  between operations  0.74 us (1%)
    ppermute x5, starting transfers between devices, both_sides(): lax.ppermute(block, 'row', [((row + 1) % rows, row) for row in range(rows)])  20.1 us
    ppermute x5, waiting for transfers between devices, both_sides(): lax.ppermute(block, 'row', [((row + 1) % rows, row) for row in range(rows)])  13.5 us
    ppermute x5, starting transfers between devices, both_sides(): lax.ppermute(block, 'row', [((row - 1) % rows, row) for row in range(rows)])  4.22 us
    pallas_call x2, Pallas kernels, with_writes(): pl.pallas_call(functools.partial(kernel, places), in_specs=specs, out_spe...  4.19 us
    pallas_call x2, Pallas kernels, mid_part(): pl.pallas_call(functools.partial(mid_kernel, span[0], len(widths)), in_sp...  2.35 us
    pallas_call x1, Pallas kernels, banded(): pl.pallas_call(band_kernel, in_specs=[SMEM, VMEM], out_specs=VMEM, out_sh...  2.17 us
    ppermute x5, waiting for transfers between devices, both_sides(): lax.ppermute(block, 'row', [((row - 1) % rows, row) for row in range(rows)])  1.78 us
    pallas_call x1, Pallas kernels, last_part(): pl.pallas_call(functools.partial(last_kernel, span[0], mid_start, [place...  1.66 us
  transfers between devices with their start and end apart: 10, of which 7 were waited for; matrix products, arithmetic and copies ran while one was open for 0% of the time, Pallas kernels for 17%

profile of v2, /device:TPU:0, one launch (start us, length us, event | category | flops | bytes accessed | tf_op | source)
XLA Modules:
  0.0 53.5 jit_solution(3257327268738748893)
XLA Ops:
  0.6 0.0 copy-start.6
  0.6 1.1 %slice.7.here_ref = bf16[512,256]{1,0:T(8,128)(2,1)S(1)} slice(f32[512,512]{1,0:T(8,128)} %now_ref.1), slice={[0:512], [0:256]} | slice | bytes 524288 | tf_op jit(solution)/shard_map/slice | solution.py:276
  1.7 3.1 %collective-permute-start.1 = (bf16[512,256]{1,0:T(8,128)(2,1)S(1)}, bf16[512,256]{1,0:T(8,128)(2,1)S(1)}, u32[]{:S(2)}, u32[]{:S(2)}) collective-permute-start(bf16[512,256]{1,0:T(8,128)(2,1)S(1)} %slice.7.here_ref), channel_id=1, source_target_pairs={{12,0},{0,4},{4,8},{8,12},{13,1},{1,5},{5,9},{9,13},{14,2},{2,6},{... | collective-permute-start | bytes 786440 | tf_op jit(solution)/shard_map/ppermute | solution.py:31
  4.8 2.1 %collective-permute-start = (bf16[512,256]{1,0:T(8,128)(2,1)S(1)}, bf16[512,256]{1,0:T(8,128)(2,1)S(1)}, u32[]{:S(2)}, u32[]{:S(2)}) collective-permute-start(bf16[512,256]{1,0:T(8,128)(2,1)S(1)} %slice.7.here_ref), channel_id=1, source_target_pairs={{4,0},{8,4},{12,8},{0,12},{5,1},{9,5},{13,9},{1,13},{6,2},{10,6},{... | collective-permute-start | bytes 786440 | tf_op jit(solution)/shard_map/ppermute | solution.py:30
  6.9 0.0 copy-start
  6.9 1.2 %copy-done = f32[512,512]{1,0:T(8,128)S(1)} copy-done((f32[512,512]{1,0:T(8,128)S(1)}, f32[512,512]{1,0:T(8,128)}, u32[]{:S(2)}) %copy-start) | copy-done | bytes 1048600
  8.1 0.0 copy-start.3
  8.2 0.0 copy-start.2
  8.2 0.0 copy-start.4
  8.2 0.1 collective-permute-start.5
  8.2 3.8 %collective-permute-start.4 = (bf16[512,256]{1,0:T(8,128)(2,1)S(1)}, bf16[512,256]{1,0:T(8,128)(2,1)S(1)}, u32[]{:S(2)}, u32[]{:S(2)}) collective-permute-start(bf16[512,256]{1,0:T(8,128)(2,1)S(1)} %round_part.1.here_ref), channel_id=1, source_target_pairs={{4,0},{8,4},{12,8},{0,12},{5,1},{9,5},{13,9},{1,13},{6,2},{10,6},{... | collective-permute-start | bytes 786440 | tf_op jit(solution)/shard_map/ppermute | solution.py:30
  12.1 0.0 copy-done.6
  12.1 0.0 copy-done.3
  12.1 2.2 %band.1.band_ref.refs_2_ = bf16[512,1536]{1,0:T(8,128)(2,1)S(1)} custom-call(s32[8,16]{1,0:T(8,128)S(1)} %copy-done.6, bf16[8,64,1024]{2,1,0:T(8,128)(2,1)S(1)} %copy-done.3), custom_call_target="tpu_custom_call" | custom-call | flops 6291456 | bytes 2621440 | tf_op jit(solution)/shard_map/band/pallas_call | solution.py:89
  14.2 0.0 collective-permute-done.1.first_ref
  14.2 5.5 %collective-permute-done.second_ref = bf16[512,256]{1,0:T(8,128)(2,1)S(1)} collective-permute-done((bf16[512,256]{1,0:T(8,128)(2,1)S(1)}, bf16[512,256]{1,0:T(8,128)(2,1)S(1)}, u32[]{:S(2)}, u32[]{:S(2)}) %collective-permute-start) | collective-permute-done | bytes 262176 | tf_op jit(solution)/shard_map/ppermute | solution.py:30
  19.8 0.0 copy-done.2
  19.8 0.0 copy-done.4
  19.8 1.2 %mid_part.2 = (f32[512,256]{1,0:T(8,128)S(1)}, bf16[512,256]{1,0:T(8,128)(2,1)S(1)}) custom-call(s32[8,8]{1,0:T(8,128)S(1)} %copy-done.4, bf16[512,1536]{1,0:T(8,128)(2,1)S(1)} %band.1.band_ref.refs_2_, bf16[512,256]{1,0:T(8,128)(2,1)S(1)} %slice.7.here_ref, bf16[512,256]{1,0:T(8,128)(2,1)S(1)} %collective-permute-done.second_ref, ...), custom_call_target="tpu_custom_call" | custom-call | flops 402653184 | bytes 3670016 | tf_op jit(solution)/shard_map/mid_part/pallas_call | solution.py:149
  21.0 0.5 collective-permute-start.3
  21.5 3.4 %collective-permute-start.2 = (bf16[512,256]{1,0:T(8,128)(2,1)S(1)}, bf16[512,256]{1,0:T(8,128)(2,1)S(1)}, u32[]{:S(2)}, u32[]{:S(2)}) collective-permute-start(bf16[512,256]{1,0:T(8,128)(2,1)S(1)} %get-tuple-element.24.refs_3_), channel_id=1, source_target_pairs={{4,0},{8,4},{12,8},{0,12},{5,1},{9,5},{13,9},{1,13},{6,2},{10,6},{... | collective-permute-start | bytes 786440 | tf_op jit(solution)/shard_map/ppermute | solution.py:30
  24.8 0.4 collective-permute-done.5.first_ref
  25.3 5.7 %collective-permute-done.4.second_ref = bf16[512,256]{1,0:T(8,128)(2,1)S(1)} collective-permute-done((bf16[512,256]{1,0:T(8,128)(2,1)S(1)}, bf16[512,256]{1,0:T(8,128)(2,1)S(1)}, u32[]{:S(2)}, u32[]{:S(2)}) %collective-permute-start.4) | collective-permute-done | bytes 262176 | tf_op jit(solution)/shard_map/ppermute | solution.py:30
  31.0 0.0 copy-start.1
  31.0 0.0 copy-start.5
  31.0 1.2 %mid_part.3 = (f32[512,256]{1,0:T(8,128)S(1)}, bf16[512,128]{1,0:T(8,128)(2,1)S(1)}, bf16[512,128]{1,0:T(8,128)(2,1)S(1)}) custom-call(s32[8,8]{1,0:T(8,128)S(1)} %copy-done.4, bf16[512,1536]{1,0:T(8,128)(2,1)S(1)} %band.1.band_ref.refs_2_, bf16[512,256]{1,0:T(8,128)(2,1)S(1)} %round_part.1.here_ref, bf16[512,256]{1,0:T(8,128)(2,1)S(1)} %collective-permute-done.4.second_ref, ...), custom_call_target="tpu_custom_call" | custom-call | flops 402653184 | bytes 3670016 | tf_op jit(solution)/shard_map/mid_part/pallas_call | solution.py:149
  32.2 0.6 %collective-permute-start.9 = (bf16[512,128]{1,0:T(8,128)(2,1)S(1)}, bf16[512,128]{1,0:T(8,128)(2,1)S(1)}, u32[]{:S(2)}, u32[]{:S(2)}) collective-permute-start(bf16[512,128]{1,0:T(8,128)(2,1)S(1)} %get-tuple-element.30.refs_3_), channel_id=1, source_target_pairs={{12,0},{0,4},{4,8},{8,12},{13,1},{1,5},{5,9},{9,13},{14,2},{2,6},{... | collective-permute-start | bytes 393224 | tf_op jit(solution)/shard_map/ppermute | solution.py:31
  32.7 3.3 %collective-permute-start.8 = (bf16[512,128]{1,0:T(8,128)(2,1)S(1)}, bf16[512,128]{1,0:T(8,128)(2,1)S(1)}, u32[]{:S(2)}, u32[]{:S(2)}) collective-permute-start(bf16[512,128]{1,0:T(8,128)(2,1)S(1)} %get-tuple-element.30.refs_3_), channel_id=1, source_target_pairs={{4,0},{8,4},{12,8},{0,12},{5,1},{9,5},{13,9},{1,13},{6,2},{10,6},{... | collective-permute-start | bytes 393224 | tf_op jit(solution)/shard_map/ppermute | solution.py:30
  36.0 0.0 collective-permute-start.7
  36.0 0.5 collective-permute-done.3.refs_5_
  36.6 7.5 %collective-permute-start.6 = (bf16[512,128]{1,0:T(8,128)(2,1)S(1)}, bf16[512,128]{1,0:T(8,128)(2,1)S(1)}, u32[]{:S(2)}, u32[]{:S(2)}) collective-permute-start(bf16[512,128]{1,0:T(8,128)(2,1)S(1)} %get-tuple-element.29.here_ref), channel_id=1, source_target_pairs={{4,0},{8,4},{12,8},{0,12},{5,1},{9,5},{13,9},{1,13},{6,2},{10,6},{... | collective-permute-start | bytes 393224 | tf_op jit(solution)/shard_map/ppermute | solution.py:30
  44.1 0.0 collective-permute-done.2.refs_4_
  44.1 0.0 copy-done.1
  44.1 0.0 copy-done.5
  44.1 2.1 %next_part.2 = (f32[512,256]{1,0:T(8,128)S(1)}, f32[512,256]{1,0:T(8,128)S(1)}, f32[512,512]{1,0:T(8,128)}) custom-call(s32[8,8]{1,0:T(8,128)S(1)} %copy-done.4, f32[2]{0:T(128)S(1)} %copy-done.5, bf16[512,1536]{1,0:T(8,128)(2,1)S(1)} %band.1.band_ref.refs_2_, bf16[512,256]{1,0:T(8,128)(2,1)S(1)} %get-tuple-element.24.refs_3_, ...), custom_call_target="tpu_custom_call" | custom-call | flops 402653184 | bytes 3061841 | tf_op jit(solution)/shard_map/next_part/pallas_call | solution.py:192
  46.2 0.0 collective-permute-done.9.refs_5_
  46.2 1.5 %collective-permute-done.8.refs_4_ = bf16[512,128]{1,0:T(8,128)(2,1)S(1)} collective-permute-done((bf16[512,128]{1,0:T(8,128)(2,1)S(1)}, bf16[512,128]{1,0:T(8,128)(2,1)S(1)}, u32[]{:S(2)}, u32[]{:S(2)}) %collective-permute-start.8) | collective-permute-done | bytes 131104 | tf_op jit(solution)/shard_map/ppermute | solution.py:30
  47.8 2.1 %next_part.3 = (f32[512,128]{1,0:T(8,128)S(1)}, f32[512,128]{1,0:T(8,128)S(1)}, f32[512,512]{1,0:T(8,128)}, f32[512,512]{1,0:T(8,128)}) custom-call(s32[8,8]{1,0:T(8,128)S(1)} %copy-done.4, f32[2]{0:T(128)S(1)} %copy-done.5, bf16[512,1536]{1,0:T(8,128)(2,1)S(1)} %band.1.band_ref.refs_2_, bf16[512,128]{1,0:T(8,128)(2,1)S(1)} %get-tuple-element.30.refs_3_, ...), custom_call_target="tpu_custom_call" | custom-call | flops 201326592 | bytes 2055208 | tf_op jit(solution)/shard_map/next_part/pallas_call | solution.py:192
  49.9 0.8 %collective-permute-done.7.first_ref = bf16[512,128]{1,0:T(8,128)(2,1)S(1)} collective-permute-done((bf16[512,128]{1,0:T(8,128)(2,1)S(1)}, bf16[512,128]{1,0:T(8,128)(2,1)S(1)}, u32[]{:S(2)}, u32[]{:S(2)}) %collective-permute-start.7) | collective-permute-done | bytes 131104 | tf_op jit(solution)/shard_map/ppermute | solution.py:31
  50.7 0.4 begun_part.1.sums_ref
  51.1 0.8 %collective-permute-done.6.second_ref = bf16[512,128]{1,0:T(8,128)(2,1)S(1)} collective-permute-done((bf16[512,128]{1,0:T(8,128)(2,1)S(1)}, bf16[512,128]{1,0:T(8,128)(2,1)S(1)}, u32[]{:S(2)}, u32[]{:S(2)}) %collective-permute-start.6) | collective-permute-done | bytes 131104 | tf_op jit(solution)/shard_map/ppermute | solution.py:30
  51.9 1.7 %last_part.1 = (f32[512,512]{1,0:T(8,128)}, f32[512,512]{1,0:T(8,128)}) custom-call(s32[8,8]{1,0:T(8,128)S(1)} %copy-done.4, f32[2]{0:T(128)S(1)} %copy-done.5, bf16[512,1536]{1,0:T(8,128)(2,1)S(1)} %band.1.band_ref.refs_2_, bf16[512,128]{1,0:T(8,128)(2,1)S(1)} %collective-permute-done.6.second_ref, ...), custom_call_target="tpu_custom_call", output_to_operand_aliasing={{0}: (8, {}), {1}: (9, {})} | custom-call | flops 67108864 | bytes 1966080 | tf_op jit(solution)/shard_map/last_part/pallas_call | solution.py:259
  (1 shorter events, 0.0 us)
Async XLA Ops:
  0.6 11.4 %copy-start.6 = (s32[8,16]{1,0:T(8,128)S(1)}, s32[8,16]{1,0:T(8,128)}, u32[]{:S(2)}) copy-start(s32[8,16]{1,0:T(8,128)} %slots_ref.1) | copy-start | bytes 1540
  1.7 12.5 %collective-permute-start.1 = (bf16[512,256]{1,0:T(8,128)(2,1)S(1)}, bf16[512,256]{1,0:T(8,128)(2,1)S(1)}, u32[]{:S(2)}, u32[]{:S(2)}) collective-permute-start(bf16[512,256]{1,0:T(8,128)(2,1)S(1)} %slice.7.here_ref), channel_id=1, source_target_pairs={{12,0},{0,4},{4,8},{8,12},{13,1},{1,5},{5,9},{9,13},{14,2},{2,6},{... | collective-permute-start | bytes 786440 | tf_op jit(solution)/shard_map/ppermute | solution.py:31
  4.8 15.0 %collective-permute-start = (bf16[512,256]{1,0:T(8,128)(2,1)S(1)}, bf16[512,256]{1,0:T(8,128)(2,1)S(1)}, u32[]{:S(2)}, u32[]{:S(2)}) collective-permute-start(bf16[512,256]{1,0:T(8,128)(2,1)S(1)} %slice.7.here_ref), channel_id=1, source_target_pairs={{4,0},{8,4},{12,8},{0,12},{5,1},{9,5},{13,9},{1,13},{6,2},{10,6},{... | collective-permute-start | bytes 786440 | tf_op jit(solution)/shard_map/ppermute | solution.py:30
  6.9 1.2 %copy-start = (f32[512,512]{1,0:T(8,128)S(1)}, f32[512,512]{1,0:T(8,128)}, u32[]{:S(2)}) copy-start(f32[512,512]{1,0:T(8,128)} %now_ref.1) | copy-start | bytes 3145732
  8.1 3.9 %copy-start.3 = (bf16[8,64,1024]{2,1,0:T(8,128)(2,1)S(1)}, bf16[8,64,1024]{2,1,0:T(8,128)(2,1)}, u32[]{:S(2)}) copy-start(bf16[8,64,1024]{2,1,0:T(8,128)(2,1)} %strips_ref) | copy-start | bytes 3145732
  8.2 11.6 %copy-start.2 = (f32[512,512]{1,0:T(8,128)S(1)}, f32[512,512]{1,0:T(8,128)}, u32[]{:S(2)}) copy-start(f32[512,512]{1,0:T(8,128)} %prev_ref.1) | copy-start | bytes 3145732
  8.2 11.6 %copy-start.4 = (s32[8,8]{1,0:T(8,128)S(1)}, s32[8,8]{1,0:T(8,128)}, u32[]{:S(2)}) copy-start(s32[8,8]{1,0:T(8,128)} %mask_ref.5) | copy-start | bytes 772
  8.2 17.1 %collective-permute-start.5 = (bf16[512,256]{1,0:T(8,128)(2,1)S(1)}, bf16[512,256]{1,0:T(8,128)(2,1)S(1)}, u32[]{:S(2)}, u32[]{:S(2)}) collective-permute-start(bf16[512,256]{1,0:T(8,128)(2,1)S(1)} %round_part.1.here_ref), channel_id=1, source_target_pairs={{12,0},{0,4},{4,8},{8,12},{13,1},{1,5},{5,9},{9,13},{14,2},{2,6},{... | collective-permute-start | bytes 786440 | tf_op jit(solution)/shard_map/ppermute | solution.py:31
  8.2 22.7 %collective-permute-start.4 = (bf16[512,256]{1,0:T(8,128)(2,1)S(1)}, bf16[512,256]{1,0:T(8,128)(2,1)S(1)}, u32[]{:S(2)}, u32[]{:S(2)}) collective-permute-start(bf16[512,256]{1,0:T(8,128)(2,1)S(1)} %round_part.1.here_ref), channel_id=1, source_target_pairs={{4,0},{8,4},{12,8},{0,12},{5,1},{9,5},{13,9},{1,13},{6,2},{10,6},{... | collective-permute-start | bytes 786440 | tf_op jit(solution)/shard_map/ppermute | solution.py:30
  21.0 15.6 %collective-permute-start.3 = (bf16[512,256]{1,0:T(8,128)(2,1)S(1)}, bf16[512,256]{1,0:T(8,128)(2,1)S(1)}, u32[]{:S(2)}, u32[]{:S(2)}) collective-permute-start(bf16[512,256]{1,0:T(8,128)(2,1)S(1)} %get-tuple-element.24.refs_3_), channel_id=1, source_target_pairs={{12,0},{0,4},{4,8},{8,12},{13,1},{1,5},{5,9},{9,13},{14,2},{2,6},{... | collective-permute-start | bytes 786440 | tf_op jit(solution)/shard_map/ppermute | solution.py:31
  21.5 22.6 %collective-permute-start.2 = (bf16[512,256]{1,0:T(8,128)(2,1)S(1)}, bf16[512,256]{1,0:T(8,128)(2,1)S(1)}, u32[]{:S(2)}, u32[]{:S(2)}) collective-permute-start(bf16[512,256]{1,0:T(8,128)(2,1)S(1)} %get-tuple-element.24.refs_3_), channel_id=1, source_target_pairs={{4,0},{8,4},{12,8},{0,12},{5,1},{9,5},{13,9},{1,13},{6,2},{10,6},{... | collective-permute-start | bytes 786440 | tf_op jit(solution)/shard_map/ppermute | solution.py:30
  31.0 13.1 %copy-start.1 = (f32[512,512]{1,0:T(8,128)S(1)}, f32[512,512]{1,0:T(8,128)}, u32[]{:S(2)}) copy-start(f32[512,512]{1,0:T(8,128)} %now_ref.1) | copy-start | bytes 3145732
  31.0 13.1 %copy-start.5 = (f32[2]{0:T(128)S(1)}, f32[2]{0:T(128)}, u32[]{:S(2)}) copy-start(f32[2]{0:T(128)} %coeffs_ref.1) | copy-start | bytes 28
  32.2 14.1 %collective-permute-start.9 = (bf16[512,128]{1,0:T(8,128)(2,1)S(1)}, bf16[512,128]{1,0:T(8,128)(2,1)S(1)}, u32[]{:S(2)}, u32[]{:S(2)}) collective-permute-start(bf16[512,128]{1,0:T(8,128)(2,1)S(1)} %get-tuple-element.30.refs_3_), channel_id=1, source_target_pairs={{12,0},{0,4},{4,8},{8,12},{13,1},{1,5},{5,9},{9,13},{14,2},{2,6},{... | collective-permute-start | bytes 393224 | tf_op jit(solution)/shard_map/ppermute | solution.py:31
  32.7 15.1 %collective-permute-start.8 = (bf16[512,128]{1,0:T(8,128)(2,1)S(1)}, bf16[512,128]{1,0:T(8,128)(2,1)S(1)}, u32[]{:S(2)}, u32[]{:S(2)}) collective-permute-start(bf16[512,128]{1,0:T(8,128)(2,1)S(1)} %get-tuple-element.30.refs_3_), channel_id=1, source_target_pairs={{4,0},{8,4},{12,8},{0,12},{5,1},{9,5},{13,9},{1,13},{6,2},{10,6},{... | collective-permute-start | bytes 393224 | tf_op jit(solution)/shard_map/ppermute | solution.py:30
  36.0 14.7 %collective-permute-start.7 = (bf16[512,128]{1,0:T(8,128)(2,1)S(1)}, bf16[512,128]{1,0:T(8,128)(2,1)S(1)}, u32[]{:S(2)}, u32[]{:S(2)}) collective-permute-start(bf16[512,128]{1,0:T(8,128)(2,1)S(1)} %get-tuple-element.29.here_ref), channel_id=1, source_target_pairs={{12,0},{0,4},{4,8},{8,12},{13,1},{1,5},{5,9},{9,13},{14,2},{2,6},{... | collective-permute-start | bytes 393224 | tf_op jit(solution)/shard_map/ppermute | solution.py:31
  36.6 15.3 %collective-permute-start.6 = (bf16[512,128]{1,0:T(8,128)(2,1)S(1)}, bf16[512,128]{1,0:T(8,128)(2,1)S(1)}, u32[]{:S(2)}, u32[]{:S(2)}) collective-permute-start(bf16[512,128]{1,0:T(8,128)(2,1)S(1)} %get-tuple-element.29.here_ref), channel_id=1, source_target_pairs={{4,0},{8,4},{12,8},{0,12},{5,1},{9,5},{13,9},{1,13},{6,2},{10,6},{... | collective-permute-start | bytes 393224 | tf_op jit(solution)/shard_map/ppermute | solution.py:30

commit v3 on v1

v3 whole, which is shorter than its diff:
```python
import functools

import jax
import jax.numpy as jnp
from jax import lax
from jax.experimental import pallas as pl
from jax.experimental.pallas import tpu as pltpu
from jax.sharding import PartitionSpec as P

LANES = 128
CHUNKS = 2
MIB = 1024 * 1024

SMEM = pl.BlockSpec(memory_space=pltpu.SMEM)
VMEM = pl.BlockSpec(memory_space=pltpu.VMEM)
ANY = pl.BlockSpec(memory_space=pl.ANY)
HBM = pl.BlockSpec(memory_space=pltpu.HBM)


def slots_of(blocks):
    first, later = blocks * 11 // 32, blocks * 9 // 32
    return first, later, later, blocks - first - 2 * later


def both_sides(block):
    rows = lax.axis_size("row")
    second = lax.ppermute(block, "row", [((row + 1) % rows, row) for row in range(rows)])
    first = lax.ppermute(block, "row", [((row - 1) % rows, row) for row in range(rows)])
    return first, second


def side_columns(depth, order):
    return pl.ds(2 * depth * order, depth)


def params(limit=32 * MIB):
    return pltpu.CompilerParams(vmem_limit_bytes=limit)


def cost(flops, moved):
    return pl.CostEstimate(flops=flops, transcendentals=0, bytes_accessed=moved)


def round_kernel(starts, now_ref, *out_refs):
    for start, out_ref in zip(starts, out_refs):
        out_ref[...] = now_ref[:, start:start + out_ref.shape[1]].astype(jnp.bfloat16)


def rounded(now, spans):
    rows = now.shape[0]
    size = rows * sum(width for _, width in spans)
    return list(pl.pallas_call(
        functools.partial(round_kernel, [start for start, _ in spans]),
        in_specs=[VMEM],
        out_specs=[VMEM] * len(spans),
        out_shape=[jax.ShapeDtypeStruct((rows, width), jnp.bfloat16) for _, width in spans],
        compiler_params=params(),
        cost_estimate=cost(size, 6 * size),
        name="round_part",
    )(now))


def band_kernel(slots_ref, strips_ref, out_ref):
    block_rows, block, slot_lanes = strips_ref.shape
    out_ref[...] = jnp.zeros_like(out_ref)
    half = lax.broadcasted_iota(jnp.int32, (block, LANES), 1) // block

    @pl.loop(0, block_rows)
    def _(row):
        at = pl.ds(pl.multiple_of(row * block, block), block)
        for pair in range(slot_lanes // LANES):
            straight = strips_ref[row, :, pair * LANES:(pair + 1) * LANES].astype(jnp.float32)
            swapped = jnp.concatenate([straight[:, block:], straight[:, :block]], axis=1)
            for side in range(2):
                target = slots_ref[row, 2 * pair + side]
                odd = target % 2
                value = jnp.where(odd == side, straight, swapped)
                value = jnp.where(half == odd, value, 0.0).astype(jnp.bfloat16)
                lanes = pl.ds(pl.multiple_of((target // 2) * LANES, LANES), LANES)
                out_ref[at, lanes] += value


def banded(h_slots, h_strips):
    block_rows, block, slot_lanes = h_strips.shape
    rows, columns = block_rows * block, 3 * block_rows * block
    return pl.pallas_call(
        band_kernel,
        in_specs=[SMEM, VMEM],
        out_specs=VMEM,
        out_shape=jax.ShapeDtypeStruct((rows, columns), jnp.bfloat16),
        compiler_params=params(),
        cost_estimate=cost(8 * rows * columns, 2 * rows * (columns + slot_lanes)),
        name="band",
    )(h_slots, h_strips)


def product(band_ref, here_ref, first_ref, second_ref=None):
    depth = here_ref.shape[0]
    total = jnp.dot(band_ref[:, depth:2 * depth], here_ref[...], preferred_element_type=jnp.float32)
    total += jnp.dot(band_ref[:, side_columns(depth, 0)], first_ref[...], preferred_element_type=jnp.float32)
    if second_ref is not None:
        total += jnp.dot(band_ref[:, side_columns(depth, 1)], second_ref[...], preferred_element_type=jnp.float32)
    return total


def kept(mask_ref, block_row, first, block, width):
    column = lax.broadcasted_iota(jnp.int32, (block, width), 1) // block
    row = jnp.zeros((block, width), jnp.int32)
    for c in range(width // block):
        row = jnp.where(column == c, mask_ref[block_row, first + c], row)
    return row != 0


def masked(start, mask_ref, term):
    rows, width = term.shape
    block = rows // mask_ref.shape[0]
    for i in range(rows // block):
        at = slice(i * block, (i + 1) * block)
        yield at, jnp.where(kept(mask_ref, i, start // block, block, width), term[at], 0.0)


def rows_of(slots, block):
    return slots // 2 * block


def half_mask_sum(mask_ref, columns):
    total = jnp.int32(0)
    for i in range(mask_ref.shape[0]):
        for c in columns:
            total += mask_ref[i, c]
    return total


def swapped(value, block):
    return jnp.concatenate([value[:, block:], value[:, :block]], axis=1)


def mid_kernel(half, slots, mask_ref, band_ref, here_ref, second_ref, first_ref, prev_ref, *rest):
    rows, width = here_ref.shape
    block = rows // mask_ref.shape[0]
    wide = width // block
    if half == 0:
        mid_ref, dense_ref, sent_ref, left_ref, packed = rest[-5:]
        packed[...] = jnp.zeros_like(packed)
        slot = jnp.int32(0)
    else:
        left_ref = rest[0]
        mid_ref, dense_ref, sent_ref, later_ref, spare_ref, packed = rest[-6:]
        packed[...] = jnp.zeros_like(packed)
        packed[:left_ref.shape[0], :] = left_ref[...]
        slot = jnp.maximum(half_mask_sum(mask_ref, range(wide)) - slots[0], 0)
    total = product(band_ref, here_ref, first_ref, second_ref)
    start = half * width
    term = 2.0 * total - prev_ref[:, start:start + width]
    side = lax.broadcasted_iota(jnp.int32, (block, LANES), 1) // block
    for i, (at, value) in enumerate(masked(start, mask_ref, term)):
        mid_ref[at, :] = value
        dense_ref[at, :] = value.astype(jnp.bfloat16)
        for group in range(width // LANES):
            straight = value[:, group * LANES:(group + 1) * LANES]
            turned = swapped(straight, block)
            for h in range(LANES // block):
                odd = slot % 2
                piece = jnp.where(side == odd, jnp.where(odd == h, straight, turned), 0.0)
                packed[pl.ds(pl.multiple_of(slot // 2 * block, block), block), :] += piece.astype(jnp.bfloat16)
                slot = slot + mask_ref[i, start // block + group * (LANES // block) + h]
    cut = 0
    for out_ref in ((sent_ref, left_ref) if half == 0 else (sent_ref, later_ref, spare_ref)):
        out_ref[...] = packed[cut:cut + out_ref.shape[0], :]
        cut += out_ref.shape[0]


def mid_part(half, slots, mask, band, here, first, second, prev, after):
    rows, width = here.shape
    block = rows // mask.shape[0]
    lists = [slots[0], sum(slots) // 2 - slots[0]] if half == 0 else list(slots[1:])
    packed = [jax.ShapeDtypeStruct((rows_of(count, block), LANES), jnp.bfloat16) for count in lists]
    return pl.pallas_call(
        functools.partial(mid_kernel, half, slots),
        in_specs=[SMEM] + [VMEM] * (5 + len(after)),
        out_specs=[VMEM] * (2 + len(packed)),
        out_shape=[
            jax.ShapeDtypeStruct(here.shape, jnp.float32), jax.ShapeDtypeStruct(here.shape, jnp.bfloat16)] + packed,
        scratch_shapes=[pltpu.VMEM((rows_of(sum(lists), block), LANES), jnp.bfloat16)],
        compiler_params=params(),
        cost_estimate=cost(6 * rows * rows * width, 6 * rows * rows + 20 * rows * width),
        name="mid_part",
    )(mask, band, here, second, first, prev, *after)


def unpacked(half, slots, mask_ref, list_refs, gathered, dense):
    rows, width = dense.shape
    block = rows // mask_ref.shape[0]
    wide = width // block
    cut = 0
    for list_ref in list_refs:
        size = min(list_ref.shape[0], gathered.shape[0] - cut)
        gathered[cut:cut + size, :] = list_ref[:size, :]
        cut += size
    slot = jnp.int32(0) if half == 0 else jnp.maximum(half_mask_sum(mask_ref, range(wide)) - slots[0], 0)
    side = lax.broadcasted_iota(jnp.int32, (block, LANES), 1) // block
    for i in range(rows // block):
        for group in range(width // LANES):
            value = jnp.zeros((block, LANES), jnp.float32)
            for h in range(LANES // block):
                held = gathered[pl.ds(pl.multiple_of(slot // 2 * block, block), block), :].astype(jnp.float32)
                keep = mask_ref[i, half * wide + group * (LANES // block) + h]
                piece = jnp.where(slot % 2 == h, held, swapped(held, block))
                value = jnp.where((side == h) & (keep != 0), piece, value)
                slot = slot + keep
            dense[i * block:(i + 1) * block, group * LANES:(group + 1) * LANES] = value.astype(jnp.bfloat16)


def next_kernel(slots, mask_ref, first_mask_ref, second_mask_ref, coeffs_ref, band_ref, here_ref, sent_first_ref,
                later_first_ref, sent_second_ref, later_second_ref, now_ref, mid_ref, other_mid_ref, *rest):
    next_ref, density_ref, out_ref, gathered, dense_first, dense_second, sems = rest[-7:]
    width = here_ref.shape[1]
    copies = []
    for p, held in enumerate((mid_ref, other_mid_ref)):
        copies.append(pltpu.make_async_copy(held, out_ref.at[:, pl.ds(p * width, width)], sems.at[p]))
        copies[-1].start()
    unpacked(0, slots, first_mask_ref, (sent_first_ref, later_first_ref), gathered, dense_first)
    unpacked(0, slots, second_mask_ref, (sent_second_ref, later_second_ref), gathered, dense_second)
    term = 2.0 * product(band_ref, here_ref, dense_first, dense_second) - now_ref[:, :width]
    for at, value in masked(0, mask_ref, term):
        next_ref[at, :] = value
        density_ref[at, :] = coeffs_ref[0] * mid_ref[at, :] + coeffs_ref[1] * value
    for copy in copies:
        copy.wait()


def next_part(slots, mask, masks, coeffs, band, here, lists, now, mids):
    rows, width = here.shape
    block = rows // mask.shape[0]
    half_rows = rows_of(sum(slots) // 2, block)
    return pl.pallas_call(
        functools.partial(next_kernel, slots),
        in_specs=[SMEM] * 4 + [VMEM] * (5 + len(lists)),
        out_specs=[VMEM] * 2 + [HBM],
        out_shape=[jax.ShapeDtypeStruct(here.shape, jnp.float32)] * 2 + [jax.ShapeDtypeStruct(now.shape, jnp.float32)],
        scratch_shapes=[
            pltpu.VMEM((half_rows, LANES), jnp.bfloat16), pltpu.VMEM(here.shape, jnp.bfloat16),
            pltpu.VMEM(here.shape, jnp.bfloat16), pltpu.SemaphoreType.DMA((2,))],
        compiler_params=params(),
        cost_estimate=cost(6 * rows * rows * width, 6 * rows * rows + 40 * rows * width),
        name="next_part",
    )(mask, *masks, coeffs, band, here, *lists, now, *mids)


def begun_kernel(slots, mask_ref, band_ref, here_ref, sent_ref, later_ref, spare_ref, now_ref, held_next_ref,
                 held_density_ref, *rest):
    next_ref, density_ref, sums_ref, gathered, dense, sems = rest[-6:]
    width = here_ref.shape[1]
    copies = []
    for held, out_ref in ((held_next_ref, next_ref), (held_density_ref, density_ref)):
        copies.append(pltpu.make_async_copy(held, out_ref.at[:, pl.ds(0, width)], sems.at[len(copies)]))
        copies[-1].start()
    unpacked(1, slots, mask_ref, (sent_ref, later_ref, spare_ref), gathered, dense)
    sums_ref[...] = 2.0 * product(band_ref, here_ref, dense) - now_ref[:, width:2 * width]
    for copy in copies:
        copy.wait()


def begun_part(slots, mask, band, here, lists, now, helds):
    rows, width = here.shape
    block = rows // mask.shape[0]
    return pl.pallas_call(
        functools.partial(begun_kernel, slots),
        in_specs=[SMEM] + [VMEM] * (5 + len(lists)),
        out_specs=[HBM] * 2 + [VMEM],
        out_shape=[jax.ShapeDtypeStruct(now.shape, jnp.float32)] * 2 + [jax.ShapeDtypeStruct(here.shape, jnp.float32)],
        scratch_shapes=[
            pltpu.VMEM((rows_of(sum(slots[1:]), block), LANES), jnp.bfloat16), pltpu.VMEM(here.shape, jnp.bfloat16),
            pltpu.SemaphoreType.DMA((2,))],
        compiler_params=params(),
        cost_estimate=cost(4 * rows * rows * width, 4 * rows * rows + 20 * rows * width),
        name="begun_part",
    )(mask, band, here, *lists, now, *helds)


def last_kernel(slots, mask_ref, side_mask_ref, coeffs_ref, band_ref, sent_ref, later_ref, spare_ref, sums_ref, mid_ref,
                *rest):
    next_ref, density_ref, gathered, dense, held_next, held_density, sems = rest[-7:]
    unpacked(1, slots, side_mask_ref, (sent_ref, later_ref, spare_ref), gathered, dense)
    rows, width = dense.shape
    block = rows // mask_ref.shape[0]
    step = rows // CHUNKS
    copies = []
    for c in range(CHUNKS):
        total = jnp.dot(
            band_ref[c * step:(c + 1) * step, side_columns(rows, 1)], dense[...], preferred_element_type=jnp.float32)
        for i in range(step // block):
            at = slice(c * step + i * block, c * step + (i + 1) * block)
            keep = kept(mask_ref, c * (step // block) + i, width // block, block, width)
            value = jnp.where(keep, 2.0 * total[i * block:(i + 1) * block] + sums_ref[at, :], 0.0)
            held_next[at, :] = value
            held_density[at, :] = coeffs_ref[0] * mid_ref[at, :] + coeffs_ref[1] * value
        done = pl.ds(c * step, step)
        for held, out_ref in ((held_next, next_ref), (held_density, density_ref)):
            copies.append(pltpu.make_async_copy(
                held.at[done, :], out_ref.at[done, pl.ds(width, width)], sems.at[len(copies)]))
            copies[-1].start()
    for copy in copies:
        copy.wait()


def last_part(slots, mask, side_mask, coeffs, band, lists, sums, mid, outs):
    rows, width = sums.shape
    block = rows // mask.shape[0]
    operands = [mask, side_mask, coeffs, band, *lists, sums, mid, *outs]
    return pl.pallas_call(
        functools.partial(last_kernel, slots),
        in_specs=[SMEM] * 3 + [VMEM] * (3 + len(lists)) + [HBM] * 2,
        out_specs=[HBM] * 2,
        out_shape=[jax.ShapeDtypeStruct(out.shape, jnp.float32) for out in outs],
        scratch_shapes=[
            pltpu.VMEM((rows_of(sum(slots[1:]), block), LANES), jnp.bfloat16),
            pltpu.VMEM((rows, width), jnp.bfloat16), pltpu.VMEM((rows, width), jnp.float32),
            pltpu.VMEM((rows, width), jnp.float32), pltpu.SemaphoreType.DMA((2 * CHUNKS,))],
        input_output_aliases={len(operands) - 2: 0, len(operands) - 1: 1},
        compiler_params=params(),
        cost_estimate=cost(2 * rows * rows * width, 2 * rows * rows + 24 * rows * width),
        name="last_part",
    )(*operands)


def neighbour_masks(t_mask, slots):
    axes = ("grp", "row", "col", "rep")
    masks = lax.all_gather(t_mask, axes)
    wide = t_mask.shape[1] // 2
    early = jnp.sum(masks[:, :, :wide], axis=(1, 2))
    late = jnp.sum(masks[:, :, wide:], axis=(1, 2))
    crowded = jnp.max(jnp.maximum(early, slots[0]) + late) > sum(slots[:3])
    rows = lax.axis_size("row")
    inner = lax.axis_size("col") * lax.axis_size("rep")
    row, rest = lax.axis_index("row"), lax.axis_index("col") * lax.axis_size("rep") + lax.axis_index("rep")
    found = []
    for turn in (-1, 1):
        at = (lax.axis_index("grp") * rows + (row + turn) % rows) * inner + rest
        found.append(lax.dynamic_index_in_dim(masks, at, keepdims=False))
    return found, crowded


def local(h_strips, h_slots, t_prev, t_now, t_mask, coeffs):
    slots = slots_of(t_mask.size)
    width = t_now.shape[1] // 2
    low = t_now[:, :width].astype(jnp.bfloat16)
    low, t_now, t_prev, h_strips = lax.optimization_barrier((low, t_now, t_prev, h_strips))
    (high,) = rounded(t_now, [(width, width)])
    masks, crowded = neighbour_masks(t_mask, slots)
    band = banded(h_slots, h_strips)
    low_sides, high_sides = both_sides(low), both_sides(high)
    mid_low, dense_low, sent_low, left = mid_part(0, slots, t_mask, band, low, *low_sides, t_prev, [])
    first_low, second_low = both_sides(sent_low)
    mid_high, dense_high, sent, later, spare = mid_part(1, slots, t_mask, band, high, *high_sides, t_prev, [left])
    first_sent, second_sent = both_sides(sent)
    first_later, second_later = both_sides(later)
    first_spare, second_spare = lax.cond(
        crowded, both_sides, lambda block: (jnp.zeros_like(block), jnp.zeros_like(block)), spare)
    next_low, density_low, t_mid = next_part(
        slots, t_mask, masks, coeffs, band, dense_low, [first_low, first_sent, second_low, second_sent], t_now,
        [mid_low, mid_high])
    *outs, sums = begun_part(
        slots, masks[0], band, dense_high, [first_sent, first_later, first_spare], t_now, [next_low, density_low])
    outs = last_part(
        slots, t_mask, masks[1], coeffs, band, [second_sent, second_later, second_spare], sums, mid_high, outs)
    return (t_mid, outs[0], outs[1])


def solution(mesh):
    panel = P(("grp", "row"), ("col", "rep"))
    return jax.shard_map(
        local,
        mesh=mesh,
        in_specs=(P(("grp", "row"), None, None), P(("grp", "row"), None), panel, panel, panel, P()),
        out_specs=(panel, panel, panel),
        check_vma=False,
    )
```

time: 53.7 us -> 94.8 us (1.77)
  blocking collectives: 0 us -> 48.1 us
  starting transfers between devices: 31.9 us -> 15.6 us
  local copies, waits for them, and re-layouts: 2.9 us -> 7.63 us
  waiting for transfers between devices: 2.81 us -> 5.54 us
  other arithmetic: 0 us -> 1.96 us
    all_gather x0 -> x1, blocking collectives: none -> 48.1 us  [neighbour_masks(): masks = lax.all_gather(t_mask, axes)]
    ppermute x16 -> x10, starting transfers between devices: 31.9 us -> 15.6 us  [the longest x5 10.2 us: both_sides(): lax.ppermute(block, 'row', [((row + 1) % rows, row) for row in range(rows)])]
    ppermute x16 -> x10, waiting for transfers between devices: 2.81 us -> 5.54 us  [the longest x5 3.91 us: both_sides(): lax.ppermute(block, 'row', [((row + 1) % rows, row) for row in range(rows)])]
    unnamed x14 -> x30, local copies, waits for them, and re-layouts: 1.93 us -> 4.61 us
    reduce_sum x0 -> x1, other arithmetic: none -> 1.27 us  [neighbour_masks(): early = jnp.sum(masks[:, :, :wide], axis=(1, 2))]
    another operation x0 -> x2, local copies, waits for them, and re-layouts: none -> 1.25 us
    pallas_call x9 -> x5, Pallas kernels: 12.7 us -> 11.9 us  [the longest x2 4.17 us: mid_part(): pl.pallas_call(functools.partial(mid_kernel, half, slots), in_specs=[SMEM...]
  transfers between devices with their start and end apart: 16 -> 10, of which waited for: 3 -> 2; matrix products, arithmetic and copies ran while one was open for 0% -> 4% of each run, Pallas kernels for 25% -> 12%
where the time goes in v3:
time: 94.8 us; the launch traced here: 94.4 us
  blocking collectives  48.1 us (51%)
  starting transfers between devices  15.6 us (16%)
  Pallas kernels  14.1 us (15%)
  local copies, waits for them, and re-layouts  7.63 us (8%)
  waiting for transfers between devices  5.54 us (6%)
  other arithmetic  1.96 us (2%)
  between operations  1.43 us (2%)
    all_gather x1, blocking collectives, neighbour_masks(): masks = lax.all_gather(t_mask, axes)  48.1 us
    ppermute x5, starting transfers between devices, both_sides(): lax.ppermute(block, 'row', [((row + 1) % rows, row) for row in range(rows)])  10.2 us
    ppermute x5, starting transfers between devices, both_sides(): lax.ppermute(block, 'row', [((row - 1) % rows, row) for row in range(rows)])  5.38 us
    unnamed x30, local copies, waits for them, and re-layouts  4.61 us
    pallas_call x2, Pallas kernels, mid_part(): pl.pallas_call(functools.partial(mid_kernel, half, slots), in_specs=[SMEM...  4.17 us
    ppermute x5, waiting for transfers between devices, both_sides(): lax.ppermute(block, 'row', [((row + 1) % rows, row) for row in range(rows)])  3.91 us
    pallas_call x1, Pallas kernels, next_part(): pl.pallas_call(functools.partial(next_kernel, slots), in_specs=[SMEM] * 4...  3.04 us
    pallas_call x1, Pallas kernels, last_part(): pl.pallas_call(functools.partial(last_kernel, slots), in_specs=[SMEM] * 3...  2.44 us
  transfers between devices with their start and end apart: 10, of which 2 were waited for; matrix products, arithmetic and copies ran while one was open for 4% of the time, Pallas kernels for 12%

profile of v3, /device:TPU:0, one launch (start us, length us, event | category | flops | bytes accessed | tf_op | source)
XLA Modules:
  0.0 94.4 jit_solution(7907143436580748922)
XLA Ops:
  0.6 0.0 copy-start.11
  0.6 1.1 %slice.19.here_ref = bf16[512,256]{1,0:T(8,128)(2,1)S(1)} slice(f32[512,512]{1,0:T(8,128)} %now_ref.2), slice={[0:512], [0:256]} | slice | bytes 524288 | tf_op jit(solution)/shard_map/slice | solution.py:347
  1.7 3.1 %collective-permute-start.3 = (bf16[512,256]{1,0:T(8,128)(2,1)S(1)}, bf16[512,256]{1,0:T(8,128)(2,1)S(1)}, u32[]{:S(2)}, u32[]{:S(2)}) collective-permute-start(bf16[512,256]{1,0:T(8,128)(2,1)S(1)} %slice.19.here_ref), channel_id=1, source_target_pairs={{12,0},{0,4},{4,8},{8,12},{13,1},{1,5},{5,9},{9,13},{14,2},{2,6},{... | collective-permute-start | bytes 786440 | tf_op jit(solution)/shard_map/ppermute | solution.py:28
  4.8 2.1 %collective-permute-start.2 = (bf16[512,256]{1,0:T(8,128)(2,1)S(1)}, bf16[512,256]{1,0:T(8,128)(2,1)S(1)}, u32[]{:S(2)}, u32[]{:S(2)}) collective-permute-start(bf16[512,256]{1,0:T(8,128)(2,1)S(1)} %slice.19.here_ref), channel_id=1, source_target_pairs={{4,0},{8,4},{12,8},{0,12},{5,1},{9,5},{13,9},{1,13},{6,2},{10,6},{... | collective-permute-start | bytes 786440 | tf_op jit(solution)/shard_map/ppermute | solution.py:27
  6.9 0.0 copy-start
  6.9 1.2 %copy-done = f32[512,512]{1,0:T(8,128)S(1)} copy-done((f32[512,512]{1,0:T(8,128)S(1)}, f32[512,512]{1,0:T(8,128)}, u32[]{:S(2)}) %copy-start) | copy-done | bytes 1048600
  8.1 0.0 copy-start.3
  8.2 0.0 copy-start.10
  8.2 0.0 copy-start.2
  8.2 0.1 collective-permute-start.6
  8.2 3.8 %collective-permute-start.5 = (bf16[512,256]{1,0:T(8,128)(2,1)S(1)}, bf16[512,256]{1,0:T(8,128)(2,1)S(1)}, u32[]{:S(2)}, u32[]{:S(2)}) collective-permute-start(bf16[512,256]{1,0:T(8,128)(2,1)S(1)} %round_part.1.here_ref), channel_id=1, source_target_pairs={{4,0},{8,4},{12,8},{0,12},{5,1},{9,5},{13,9},{1,13},{6,2},{10,6},{... | collective-permute-start | bytes 786440 | tf_op jit(solution)/shard_map/ppermute | solution.py:27
  12.1 0.0 copy-done.11
  12.1 0.0 copy-done.3
  12.1 2.2 %band.1.band_ref = bf16[512,1536]{1,0:T(8,128)(2,1)S(1)} custom-call(s32[8,16]{1,0:T(8,128)S(1)} %copy-done.11, bf16[8,64,1024]{2,1,0:T(8,128)(2,1)S(1)} %copy-done.3), custom_call_target="tpu_custom_call" | custom-call | flops 6291456 | bytes 2621440 | tf_op jit(solution)/shard_map/band/pallas_call | solution.py:86
  14.2 0.0 copy-done.10
  14.2 48.1 %all-gather = s32[256,8]{1,0:T(8,128)S(1)} all-gather(s32[8,8]{1,0:T(8,128)S(1)} %copy-done.10), channel_id=2, replica_groups=mesh['grp'=2,'row'=4,'col'=2,'rep'=2] {'grp','row','col','rep'}, dimensions={0}, use_global_device_ids=true | all-gather | bytes 8448 | tf_op jit(solution)/shard_map/all_gather | solution.py:329
  62.3 0.0 copy-start.14
  62.3 1.3 %slice_reduce_fusion.1 = (s32[32]{0:T(128)S(1)}, s32[32]{0:T(128)S(1)}) fusion(s32[32,8,8]{2,1,0:T(8,128)S(1)} %bitcast.5), kind=kLoop, calls=%fused_computation.2 | loop fusion | flops 1984 | bytes 8448 | tf_op jit(solution)/shard_map/reduce_sum | solution.py:331
  63.6 0.0 collective-permute-done.3.first_ref
  63.6 0.0 copy-done.14
  63.6 0.0 collective-permute-done.2.second_ref
  63.6 0.0 copy-done.2
  63.6 2.1 %mid_part.2 = (f32[512,256]{1,0:T(8,128)S(1)}, bf16[512,256]{1,0:T(8,128)(2,1)S(1)}, bf16[704,128]{1,0:T(8,128)(2,1)}, bf16[320,128]{1,0:T(8,128)(2,1)S(1)}) custom-call(s32[8,8]{1,0:T(8,128)S(1)} %copy-done.10, bf16[512,1536]{1,0:T(8,128)(2,1)S(1)} %band.1.band_ref, bf16[512,256]{1,0:T(8,128)(2,1)S(1)} %slice.19.here_ref, ...), custom_call_target="tpu_custom_call" | custom-call | flops 402653184 | bytes 4194304 | tf_op jit(solution)/shard_map/mid_part/pallas_call | solution.py:178
  65.7 0.0 copy-start.4
  65.7 0.0 copy-start.6
  65.7 0.0 collective-permute-start.8
  65.7 2.0 %collective-permute-start.4 = (bf16[704,128]{1,0:T(8,128)(2,1)}, bf16[704,128]{1,0:T(8,128)(2,1)}, u32[]{:S(2)}, u32[]{:S(2)}) collective-permute-start(bf16[704,128]{1,0:T(8,128)(2,1)} %get-tuple-element.31), channel_id=1, source_target_pairs={{12,0},{0,4},{4,8},{8,12},{13,1},{1,5},{5,9},{9,13},{14,2},{2,6},{... | collective-permute-start | bytes 540680 | tf_op jit(solution)/shard_map/ppermute | solution.py:28
  67.8 0.0 collective-permute-done.6.first_ref
  67.8 0.0 collective-permute-done.5.second_ref
  67.8 0.0 copy-start.1
  67.8 0.0 copy-start.12
  67.8 2.1 %mid_part.3 = (f32[512,256]{1,0:T(8,128)S(1)}, bf16[512,256]{1,0:T(8,128)(2,1)S(1)}, bf16[576,128]{1,0:T(8,128)(2,1)}, bf16[576,128]{1,0:T(8,128)(2,1)S(1)}, bf16[192,128]{1,0:T(8,128)(2,1)S(1)}) custom-call(s32[8,8]{1,0:T(8,128)S(1)} %copy-done.10, bf16[512,1536]{1,0:T(8,128)(2,1)S(1)} %band.1.band_ref, bf16[512,256]{1,0:T(8,128)(2,1)S(1)} %round_part.1.here_ref, ...), custom_call_target="tpu_custom_call" | custom-call | flops 402653184 | bytes 4194304 | tf_op jit(solution)/shard_map/mid_part/pallas_call | solution.py:178
  69.9 0.0 copy-done.4
  69.9 0.0 copy-done.6
  69.9 0.0 copy-start.8
  69.9 0.7 copy-done.8
  70.6 0.0 copy-start.13
  70.6 0.6 copy-done.13
  71.2 1.8 %collective-permute-start.9 = (bf16[576,128]{1,0:T(8,128)(2,1)}, bf16[576,128]{1,0:T(8,128)(2,1)S(1)}, u32[]{:S(2)}, u32[]{:S(2)}) collective-permute-start(bf16[576,128]{1,0:T(8,128)(2,1)} %get-tuple-element.34), channel_id=1, source_target_pairs={{4,0},{8,4},{12,8},{0,12},{5,1},{9,5},{13,9},{1,13},{6,2},{10,6},{... | collective-permute-start | bytes 442376 | tf_op jit(solution)/shard_map/ppermute | solution.py:27
  73.1 0.7 add_reduce_fusion
  74.4 1.3 %conditional.1 = (bf16[192,128]{1,0:T(8,128)(2,1)}, bf16[192,128]{1,0:T(8,128)(2,1)}) conditional(s32[]{:T(128)} %convert_element_type.4, () %tuple.18, bf16[192,128]{1,0:T(8,128)(2,1)S(1)} %get-tuple-element.39), branch_computations={%region_3.4_spmd, %region_4.5_spmd} | conditional | bytes 393312 | solution.py:358
  74.4 0.6 broadcast.4.clone
  75.0 0.6 broadcast.4
  75.7 0.2 collective-permute-start.7
  75.8 0.0 collective-permute-start.11
  75.9 3.9 %collective-permute-done.9.later_second_ref.sent_ref = bf16[576,128]{1,0:T(8,128)(2,1)S(1)} collective-permute-done((bf16[576,128]{1,0:T(8,128)(2,1)}, bf16[576,128]{1,0:T(8,128)(2,1)S(1)}, u32[]{:S(2)}, u32[]{:S(2)}) %collective-permute-start.9) | collective-permute-done | bytes 147488 | tf_op jit(solution)/shard_map/ppermute | solution.py:27
  79.8 2.5 %collective-permute-start.10 = (bf16[576,128]{1,0:T(8,128)(2,1)}, bf16[576,128]{1,0:T(8,128)(2,1)S(1)}, u32[]{:S(2)}, u32[]{:S(2)}) collective-permute-start(bf16[576,128]{1,0:T(8,128)(2,1)} %copy-done.13), channel_id=1, source_target_pairs={{4,0},{8,4},{12,8},{0,12},{5,1},{9,5},{13,9},{1,13},{6,2},{10,6},{... | collective-permute-start | bytes 442376 | tf_op jit(solution)/shard_map/ppermute | solution.py:27
  82.3 0.7 dynamic-slice_bitcast_fusion
  83.0 1.6 %collective-permute-done.7.later_first_ref.sent_ref = bf16[576,128]{1,0:T(8,128)(2,1)S(1)} collective-permute-done((bf16[576,128]{1,0:T(8,128)(2,1)}, bf16[576,128]{1,0:T(8,128)(2,1)S(1)}, u32[]{:S(2)}, u32[]{:S(2)}) %collective-permute-start.7) | collective-permute-done | bytes 147488 | tf_op jit(solution)/shard_map/ppermute | solution.py:28
  84.6 0.0 collective-permute-done.8.sent_second_ref
  84.6 0.0 collective-permute-done.4.sent_first_ref
  84.6 0.0 copy-done.1
  84.6 0.0 copy-done.12
  84.6 0.0 copy-start.5
  84.6 1.0 %copy-done.5 = f32[512,256]{1,0:T(8,128)S(1)} copy-done((f32[512,256]{1,0:T(8,128)S(1)}, f32[512,256]{1,0:T(8,128)}, u32[]{:S(2)}) %copy-start.5) | copy-done | bytes 524312
  85.7 0.0 copy-start.7
  85.7 0.9 %copy-done.7 = bf16[512,256]{1,0:T(8,128)(2,1)S(1)} copy-done((bf16[512,256]{1,0:T(8,128)(2,1)S(1)}, bf16[512,256]{1,0:T(8,128)(2,1)}, u32[]{:S(2)}) %copy-start.7) | copy-done | bytes 262168
  86.6 0.0 copy-start.9
  86.6 3.0 %next_part.1 = (f32[512,256]{1,0:T(8,128)S(1)}, f32[512,256]{1,0:T(8,128)S(1)}, f32[512,512]{1,0:T(8,128)}) custom-call(s32[8,8]{1,0:T(8,128)S(1)} %copy-done.10, s32[8,8]{1,0:T(8,128)S(1)} %get-tuple-element.53.first_mask_ref.mask_ref, s32[8,8]{1,0:T(8,128)S(1)} %get-tuple-element.52.second_mask_ref.side_mask_ref, f32[2]{0:T(128)S(1)} %copy-done.12, ...), custom_call_target="tpu_custom_call" | custom-call | flops 402653184 | bytes 6815744 | tf_op jit(solution)/shard_map/next_part/pallas_call | solution.py:236
  89.7 0.0 collective-permute-done.11.later_ref
  89.7 0.0 copy-done.9
  89.7 2.2 %begun_part.1 = (f32[512,512]{1,0:T(8,128)}, f32[512,512]{1,0:T(8,128)}, f32[512,256]{1,0:T(8,128)S(1)}) custom-call(s32[8,8]{1,0:T(8,128)S(1)} %get-tuple-element.53.first_mask_ref.mask_ref, bf16[512,1536]{1,0:T(8,128)(2,1)S(1)} %band.1.band_ref, bf16[512,256]{1,0:T(8,128)(2,1)S(1)} %copy-done.9, ...), custom_call_target="tpu_custom_call" | custom-call | flops 268435456 | bytes 3670016 | tf_op jit(solution)/shard_map/begun_part/pallas_call | solution.py:267
  91.9 0.0 collective-permute-done.10.later_ref
  91.9 2.4 %last_part.1 = (f32[512,512]{1,0:T(8,128)}, f32[512,512]{1,0:T(8,128)}) custom-call(s32[8,8]{1,0:T(8,128)S(1)} %copy-done.10, s32[8,8]{1,0:T(8,128)S(1)} %get-tuple-element.52.second_mask_ref.side_mask_ref, f32[2]{0:T(128)S(1)} %copy-done.12, bf16[512,1536]{1,0:T(8,128)(2,1)S(1)} %band.1.band_ref, ...), custom_call_target="tpu_custom_call", output_to_operand_aliasing={{0}: (9, {}), {1}: (10, {})} | custom-call | flops 134217728 | bytes 3670016 | tf_op jit(solution)/shard_map/last_part/pallas_call | solution.py:311
  (1 shorter events, 0.0 us)
Async XLA Ops:
  0.6 11.4 %copy-start.11 = (s32[8,16]{1,0:T(8,128)S(1)}, s32[8,16]{1,0:T(8,128)}, u32[]{:S(2)}) copy-start(s32[8,16]{1,0:T(8,128)} %slots_ref.1) | copy-start | bytes 1540
  1.7 61.9 %collective-permute-start.3 = (bf16[512,256]{1,0:T(8,128)(2,1)S(1)}, bf16[512,256]{1,0:T(8,128)(2,1)S(1)}, u32[]{:S(2)}, u32[]{:S(2)}) collective-permute-start(bf16[512,256]{1,0:T(8,128)(2,1)S(1)} %slice.19.here_ref), channel_id=1, source_target_pairs={{12,0},{0,4},{4,8},{8,12},{13,1},{1,5},{5,9},{9,13},{14,2},{2,6},{... | collective-permute-start | bytes 786440 | tf_op jit(solution)/shard_map/ppermute | solution.py:28
  4.8 58.8 %collective-permute-start.2 = (bf16[512,256]{1,0:T(8,128)(2,1)S(1)}, bf16[512,256]{1,0:T(8,128)(2,1)S(1)}, u32[]{:S(2)}, u32[]{:S(2)}) collective-permute-start(bf16[512,256]{1,0:T(8,128)(2,1)S(1)} %slice.19.here_ref), channel_id=1, source_target_pairs={{4,0},{8,4},{12,8},{0,12},{5,1},{9,5},{13,9},{1,13},{6,2},{10,6},{... | collective-permute-start | bytes 786440 | tf_op jit(solution)/shard_map/ppermute | solution.py:27
  6.9 1.2 %copy-start = (f32[512,512]{1,0:T(8,128)S(1)}, f32[512,512]{1,0:T(8,128)}, u32[]{:S(2)}) copy-start(f32[512,512]{1,0:T(8,128)} %now_ref.2) | copy-start | bytes 3145732
  8.1 3.9 %copy-start.3 = (bf16[8,64,1024]{2,1,0:T(8,128)(2,1)S(1)}, bf16[8,64,1024]{2,1,0:T(8,128)(2,1)}, u32[]{:S(2)}) copy-start(bf16[8,64,1024]{2,1,0:T(8,128)(2,1)} %strips_ref) | copy-start | bytes 3145732
  8.2 6.1 %copy-start.10 = (s32[8,8]{1,0:T(8,128)S(1)}, s32[8,8]{1,0:T(8,128)}, u32[]{:S(2)}) copy-start(s32[8,8]{1,0:T(8,128)} %mask_ref.7) | copy-start | bytes 772
  8.2 55.5 %copy-start.2 = (f32[512,512]{1,0:T(8,128)S(1)}, f32[512,512]{1,0:T(8,128)}, u32[]{:S(2)}) copy-start(f32[512,512]{1,0:T(8,128)} %prev_ref.1) | copy-start | bytes 3145732
  8.2 59.6 %collective-permute-start.6 = (bf16[512,256]{1,0:T(8,128)(2,1)S(1)}, bf16[512,256]{1,0:T(8,128)(2,1)S(1)}, u32[]{:S(2)}, u32[]{:S(2)}) collective-permute-start(bf16[512,256]{1,0:T(8,128)(2,1)S(1)} %round_part.1.here_ref), channel_id=1, source_target_pairs={{12,0},{0,4},{4,8},{8,12},{13,1},{1,5},{5,9},{9,13},{14,2},{2,6},{... | collective-permute-start | bytes 786440 | tf_op jit(solution)/shard_map/ppermute | solution.py:28
  8.2 59.5 %collective-permute-start.5 = (bf16[512,256]{1,0:T(8,128)(2,1)S(1)}, bf16[512,256]{1,0:T(8,128)(2,1)S(1)}, u32[]{:S(2)}, u32[]{:S(2)}) collective-permute-start(bf16[512,256]{1,0:T(8,128)(2,1)S(1)} %round_part.1.here_ref), channel_id=1, source_target_pairs={{4,0},{8,4},{12,8},{0,12},{5,1},{9,5},{13,9},{1,13},{6,2},{10,6},{... | collective-permute-start | bytes 786440 | tf_op jit(solution)/shard_map/ppermute | solution.py:27
  62.3 1.3 %copy-start.14 = (s32[256,8]{1,0:T(8,128)}, s32[256,8]{1,0:T(8,128)S(1)}, u32[]{:S(2)}) copy-start(s32[256,8]{1,0:T(8,128)S(1)} %all-gather) | copy-start | bytes 24580
  65.7 4.1 %copy-start.4 = (f32[512,256]{1,0:T(8,128)}, f32[512,256]{1,0:T(8,128)S(1)}, u32[]{:S(2)}) copy-start(f32[512,256]{1,0:T(8,128)S(1)} %get-tuple-element.35.mid_ref) | copy-start | bytes 1572868
  65.7 4.1 %copy-start.6 = (bf16[512,256]{1,0:T(8,128)(2,1)}, bf16[512,256]{1,0:T(8,128)(2,1)S(1)}, u32[]{:S(2)}) copy-start(bf16[512,256]{1,0:T(8,128)(2,1)S(1)} %get-tuple-element.30.here_ref) | copy-start | bytes 786436
  65.7 18.9 %collective-permute-start.8 = (bf16[704,128]{1,0:T(8,128)(2,1)}, bf16[704,128]{1,0:T(8,128)(2,1)}, u32[]{:S(2)}, u32[]{:S(2)}) collective-permute-start(bf16[704,128]{1,0:T(8,128)(2,1)} %get-tuple-element.31), channel_id=1, source_target_pairs={{4,0},{8,4},{12,8},{0,12},{5,1},{9,5},{13,9},{1,13},{6,2},{10,6},{... | collective-permute-start | bytes 540680 | tf_op jit(solution)/shard_map/ppermute | solution.py:27
  65.7 18.9 %collective-permute-start.4 = (bf16[704,128]{1,0:T(8,128)(2,1)}, bf16[704,128]{1,0:T(8,128)(2,1)}, u32[]{:S(2)}, u32[]{:S(2)}) collective-permute-start(bf16[704,128]{1,0:T(8,128)(2,1)} %get-tuple-element.31), channel_id=1, source_target_pairs={{12,0},{0,4},{4,8},{8,12},{13,1},{1,5},{5,9},{9,13},{14,2},{2,6},{... | collective-permute-start | bytes 540680 | tf_op jit(solution)/shard_map/ppermute | solution.py:28
  67.8 16.8 %copy-start.1 = (f32[512,512]{1,0:T(8,128)S(1)}, f32[512,512]{1,0:T(8,128)}, u32[]{:S(2)}) copy-start(f32[512,512]{1,0:T(8,128)} %now_ref.2) | copy-start | bytes 3145732
  67.8 16.8 %copy-start.12 = (f32[2]{0:T(128)S(1)}, f32[2]{0:T(128)}, u32[]{:S(2)}) copy-start(f32[2]{0:T(128)} %coeffs_ref.3) | copy-start | bytes 28
  69.9 0.7 copy-start.8
  70.6 0.7 copy-start.13
  71.2 8.5 %collective-permute-start.9 = (bf16[576,128]{1,0:T(8,128)(2,1)}, bf16[576,128]{1,0:T(8,128)(2,1)S(1)}, u32[]{:S(2)}, u32[]{:S(2)}) collective-permute-start(bf16[576,128]{1,0:T(8,128)(2,1)} %get-tuple-element.34), channel_id=1, source_target_pairs={{4,0},{8,4},{12,8},{0,12},{5,1},{9,5},{13,9},{1,13},{6,2},{10,6},{... | collective-permute-start | bytes 442376 | tf_op jit(solution)/shard_map/ppermute | solution.py:27
  75.7 8.9 %collective-permute-start.7 = (bf16[576,128]{1,0:T(8,128)(2,1)}, bf16[576,128]{1,0:T(8,128)(2,1)S(1)}, u32[]{:S(2)}, u32[]{:S(2)}) collective-permute-start(bf16[576,128]{1,0:T(8,128)(2,1)} %get-tuple-element.34), channel_id=1, source_target_pairs={{12,0},{0,4},{4,8},{8,12},{13,1},{1,5},{5,9},{9,13},{14,2},{2,6},{... | collective-permute-start | bytes 442376 | tf_op jit(solution)/shard_map/ppermute | solution.py:28
  75.8 13.8 %collective-permute-start.11 = (bf16[576,128]{1,0:T(8,128)(2,1)}, bf16[576,128]{1,0:T(8,128)(2,1)S(1)}, u32[]{:S(2)}, u32[]{:S(2)}) collective-permute-start(bf16[576,128]{1,0:T(8,128)(2,1)} %copy-done.13), channel_id=1, source_target_pairs={{12,0},{0,4},{4,8},{8,12},{13,1},{1,5},{5,9},{9,13},{14,2},{2,6},{... | collective-permute-start | bytes 442376 | tf_op jit(solution)/shard_map/ppermute | solution.py:28
  79.8 12.1 %collective-permute-start.10 = (bf16[576,128]{1,0:T(8,128)(2,1)}, bf16[576,128]{1,0:T(8,128)(2,1)S(1)}, u32[]{:S(2)}, u32[]{:S(2)}) collective-permute-start(bf16[576,128]{1,0:T(8,128)(2,1)} %copy-done.13), channel_id=1, source_target_pairs={{4,0},{8,4},{12,8},{0,12},{5,1},{9,5},{13,9},{1,13},{6,2},{10,6},{... | collective-permute-start | bytes 442376 | tf_op jit(solution)/shard_map/ppermute | solution.py:27
  84.6 1.0 %copy-start.5 = (f32[512,256]{1,0:T(8,128)S(1)}, f32[512,256]{1,0:T(8,128)}, u32[]{:S(2)}) copy-start(f32[512,256]{1,0:T(8,128)} %copy-done.4) | copy-start | bytes 1572868
  85.7 0.9 %copy-start.7 = (bf16[512,256]{1,0:T(8,128)(2,1)S(1)}, bf16[512,256]{1,0:T(8,128)(2,1)}, u32[]{:S(2)}) copy-start(bf16[512,256]{1,0:T(8,128)(2,1)} %copy-done.6) | copy-start | bytes 786436
  86.6 3.1 %copy-start.9 = (bf16[512,256]{1,0:T(8,128)(2,1)S(1)}, bf16[512,256]{1,0:T(8,128)(2,1)}, u32[]{:S(2)}) copy-start(bf16[512,256]{1,0:T(8,128)(2,1)} %copy-done.8) | copy-start | bytes 786436

commit v4 on v2

--- a/solution.py
+++ b/solution.py
@@ -26,14 +26,21 @@
 
 
 def both_sides(block):
-    rows = lax.axis_size("row")
-    second = lax.ppermute(block, "row", [((row + 1) % rows, row) for row in range(rows)])
-    first = lax.ppermute(block, "row", [((row - 1) % rows, row) for row in range(rows)])
-    return first, second
+    rows, reps = lax.axis_size("row"), lax.axis_size("rep")
+    arrived = []
+    for turn in (-1, 1):
+        route = []
+        for row in range(rows):
+            for rep in range(reps):
+                source = (row + (turn if rep % 2 == 0 else -turn)) % rows
+                route.append((source * reps + rep, row * reps + rep))
+        arrived.append(lax.ppermute(block, ("row", "rep"), route))
+    return tuple(arrived)
 
 
 def side_columns(depth, order):
-    return pl.ds(2 * depth * order, depth)
+    odd = lax.axis_index("rep") % 2
+    return pl.ds(pl.multiple_of(jnp.where(odd == order, 0, 2 * depth), LANES), depth)
 
 
 def params(limit=32 * MIB):

time: 53.7 us -> 53.4 us (level)
  waiting for transfers between devices: 15.3 us -> 13.9 us
  starting transfers between devices: 24.3 us -> 25 us
    ppermute x10, waiting for transfers between devices: 15.3 us -> 13.9 us  [both_sides(): arrived.append(lax.ppermute(block, ('row', 'rep'), route))]
    ppermute x10, starting transfers between devices: 24.3 us -> 25 us  [both_sides(): arrived.append(lax.ppermute(block, ('row', 'rep'), route))]
  transfers between devices with their start and end apart: 10 -> 10, of which waited for: 7 -> 5; matrix products, arithmetic and copies ran while one was open for 0% -> 0% of each run, Pallas kernels for 17% -> 17%
where the time goes in v4:
time: 53.4 us; the launch traced here: 52.9 us
  starting transfers between devices  25 us (47%)
  waiting for transfers between devices  13.9 us (26%)
  Pallas kernels  10.9 us (20%)
  local copies, waits for them, and re-layouts  2.33 us (4%)
  between operations  0.76 us (1%)
    ppermute x10, starting transfers between devices, both_sides(): arrived.append(lax.ppermute(block, ('row', 'rep'), route))  25 us
    ppermute x10, waiting for transfers between devices, both_sides(): arrived.append(lax.ppermute(block, ('row', 'rep'), route))  13.9 us
    pallas_call x2, Pallas kernels, with_writes(): pl.pallas_call(functools.partial(kernel, places), in_specs=specs, out_spe...  4.19 us
    pallas_call x2, Pallas kernels, mid_part(): pl.pallas_call(functools.partial(mid_kernel, span[0], len(widths)), in_sp...  2.35 us
    pallas_call x1, Pallas kernels, banded(): pl.pallas_call(band_kernel, in_specs=[SMEM, VMEM], out_specs=VMEM, out_sh...  2.17 us
    pallas_call x1, Pallas kernels, last_part(): pl.pallas_call(functools.partial(last_kernel, span[0], mid_start, [place...  1.73 us
    unnamed x14, local copies, waits for them, and re-layouts  1.25 us
    slice x1, local copies, waits for them, and re-layouts, local(): here = [t_now[:, start:start + width].astype(jnp.bfloat16)]  1.07 us
  transfers between devices with their start and end apart: 10, of which 5 were waited for; matrix products, arithmetic and copies ran while one was open for 0% of the time, Pallas kernels for 17%

profile of v4, /device:TPU:0, one launch (start us, length us, event | category | flops | bytes accessed | tf_op | source)
XLA Modules:
  0.0 52.9 jit_solution(13605312900842005649)
XLA Ops:
  0.6 0.0 copy-start.6
  0.6 1.1 %slice.7.here_ref = bf16[512,256]{1,0:T(8,128)(2,1)S(1)} slice(f32[512,512]{1,0:T(8,128)} %now_ref.1), slice={[0:512], [0:256]} | slice | bytes 524288 | tf_op jit(solution)/shard_map/slice | solution.py:283
  1.7 3.1 %collective-permute-start.1 = (bf16[512,256]{1,0:T(8,128)(2,1)S(1)}, bf16[512,256]{1,0:T(8,128)(2,1)S(1)}, u32[]{:S(2)}, u32[]{:S(2)}) collective-permute-start(bf16[512,256]{1,0:T(8,128)(2,1)S(1)} %slice.7.here_ref), channel_id=1, source_target_pairs={{12,0},{5,1},{0,4},{9,5},{4,8},{13,9},{8,12},{1,13},{14,2},{7,3},{... | collective-permute-start | bytes 786440 | tf_op jit(solution)/shard_map/ppermute | solution.py:37
  4.8 2.1 %collective-permute-start = (bf16[512,256]{1,0:T(8,128)(2,1)S(1)}, bf16[512,256]{1,0:T(8,128)(2,1)S(1)}, u32[]{:S(2)}, u32[]{:S(2)}) collective-permute-start(bf16[512,256]{1,0:T(8,128)(2,1)S(1)} %slice.7.here_ref), channel_id=1, source_target_pairs={{4,0},{13,1},{8,4},{1,5},{12,8},{5,9},{0,12},{9,13},{6,2},{15,3},{... | collective-permute-start | bytes 786440 | tf_op jit(solution)/shard_map/ppermute | solution.py:37
  6.9 0.0 copy-start
  6.9 1.2 %copy-done = f32[512,512]{1,0:T(8,128)S(1)} copy-done((f32[512,512]{1,0:T(8,128)S(1)}, f32[512,512]{1,0:T(8,128)}, u32[]{:S(2)}) %copy-start) | copy-done | bytes 1048600
  8.1 0.0 copy-start.3
  8.2 0.0 copy-start.2
  8.2 0.0 copy-start.4
  8.2 0.1 collective-permute-start.5
  8.2 3.8 %collective-permute-start.4 = (bf16[512,256]{1,0:T(8,128)(2,1)S(1)}, bf16[512,256]{1,0:T(8,128)(2,1)S(1)}, u32[]{:S(2)}, u32[]{:S(2)}) collective-permute-start(bf16[512,256]{1,0:T(8,128)(2,1)S(1)} %round_part.1.here_ref), channel_id=1, source_target_pairs={{4,0},{13,1},{8,4},{1,5},{12,8},{5,9},{0,12},{9,13},{6,2},{15,3},{... | collective-permute-start | bytes 786440 | tf_op jit(solution)/shard_map/ppermute | solution.py:37
  12.1 0.0 copy-done.6
  12.1 0.0 copy-done.3
  12.1 2.2 %band.1.band_ref.refs_2_ = bf16[512,1536]{1,0:T(8,128)(2,1)S(1)} custom-call(s32[8,16]{1,0:T(8,128)S(1)} %copy-done.6, bf16[8,64,1024]{2,1,0:T(8,128)(2,1)S(1)} %copy-done.3), custom_call_target="tpu_custom_call" | custom-call | flops 6291456 | bytes 2621440 | tf_op jit(solution)/shard_map/band/pallas_call | solution.py:96
  14.2 0.0 collective-permute-done.1.first_ref
  14.2 4.3 %collective-permute-done.second_ref = bf16[512,256]{1,0:T(8,128)(2,1)S(1)} collective-permute-done((bf16[512,256]{1,0:T(8,128)(2,1)S(1)}, bf16[512,256]{1,0:T(8,128)(2,1)S(1)}, u32[]{:S(2)}, u32[]{:S(2)}) %collective-permute-start) | collective-permute-done | bytes 262176 | tf_op jit(solution)/shard_map/ppermute | solution.py:37
  18.6 0.0 copy-done.2
  18.6 0.0 copy-done.4
  18.6 1.2 %mid_part.2 = (f32[512,256]{1,0:T(8,128)S(1)}, bf16[512,256]{1,0:T(8,128)(2,1)S(1)}) custom-call(s32[8,8]{1,0:T(8,128)S(1)} %copy-done.4, bf16[512,1536]{1,0:T(8,128)(2,1)S(1)} %band.1.band_ref.refs_2_, bf16[512,256]{1,0:T(8,128)(2,1)S(1)} %slice.7.here_ref, bf16[512,256]{1,0:T(8,128)(2,1)S(1)} %collective-permute-done.second_ref, ...), custom_call_target="tpu_custom_call" | custom-call | flops 402653184 | bytes 3670016 | tf_op jit(solution)/shard_map/mid_part/pallas_call | solution.py:156
  19.8 2.8 %collective-permute-start.3 = (bf16[512,256]{1,0:T(8,128)(2,1)S(1)}, bf16[512,256]{1,0:T(8,128)(2,1)S(1)}, u32[]{:S(2)}, u32[]{:S(2)}) collective-permute-start(bf16[512,256]{1,0:T(8,128)(2,1)S(1)} %get-tuple-element.24.refs_3_), channel_id=1, source_target_pairs={{12,0},{5,1},{0,4},{9,5},{4,8},{13,9},{8,12},{1,13},{14,2},{7,3},{... | collective-permute-start | bytes 786440 | tf_op jit(solution)/shard_map/ppermute | solution.py:37
  22.5 1.1 %collective-permute-start.2 = (bf16[512,256]{1,0:T(8,128)(2,1)S(1)}, bf16[512,256]{1,0:T(8,128)(2,1)S(1)}, u32[]{:S(2)}, u32[]{:S(2)}) collective-permute-start(bf16[512,256]{1,0:T(8,128)(2,1)S(1)} %get-tuple-element.24.refs_3_), channel_id=1, source_target_pairs={{4,0},{13,1},{8,4},{1,5},{12,8},{5,9},{0,12},{9,13},{6,2},{15,3},{... | collective-permute-start | bytes 786440 | tf_op jit(solution)/shard_map/ppermute | solution.py:37
  23.6 1.7 %collective-permute-done.5.first_ref = bf16[512,256]{1,0:T(8,128)(2,1)S(1)} collective-permute-done((bf16[512,256]{1,0:T(8,128)(2,1)S(1)}, bf16[512,256]{1,0:T(8,128)(2,1)S(1)}, u32[]{:S(2)}, u32[]{:S(2)}) %collective-permute-start.5) | collective-permute-done | bytes 262176 | tf_op jit(solution)/shard_map/ppermute | solution.py:37
  25.3 3.6 %collective-permute-done.4.second_ref = bf16[512,256]{1,0:T(8,128)(2,1)S(1)} collective-permute-done((bf16[512,256]{1,0:T(8,128)(2,1)S(1)}, bf16[512,256]{1,0:T(8,128)(2,1)S(1)}, u32[]{:S(2)}, u32[]{:S(2)}) %collective-permute-start.4) | collective-permute-done | bytes 262176 | tf_op jit(solution)/shard_map/ppermute | solution.py:37
  28.9 0.0 copy-start.1
  28.9 0.0 copy-start.5
  28.9 1.2 %mid_part.3 = (f32[512,256]{1,0:T(8,128)S(1)}, bf16[512,128]{1,0:T(8,128)(2,1)S(1)}, bf16[512,128]{1,0:T(8,128)(2,1)S(1)}) custom-call(s32[8,8]{1,0:T(8,128)S(1)} %copy-done.4, bf16[512,1536]{1,0:T(8,128)(2,1)S(1)} %band.1.band_ref.refs_2_, bf16[512,256]{1,0:T(8,128)(2,1)S(1)} %round_part.1.here_ref, bf16[512,256]{1,0:T(8,128)(2,1)S(1)} %collective-permute-done.4.second_ref, ...), custom_call_target="tpu_custom_call" | custom-call | flops 402653184 | bytes 3670016 | tf_op jit(solution)/shard_map/mid_part/pallas_call | solution.py:156
  30.1 2.6 %collective-permute-start.9 = (bf16[512,128]{1,0:T(8,128)(2,1)S(1)}, bf16[512,128]{1,0:T(8,128)(2,1)S(1)}, u32[]{:S(2)}, u32[]{:S(2)}) collective-permute-start(bf16[512,128]{1,0:T(8,128)(2,1)S(1)} %get-tuple-element.30.refs_3_), channel_id=1, source_target_pairs={{12,0},{5,1},{0,4},{9,5},{4,8},{13,9},{8,12},{1,13},{14,2},{7,3},{... | collective-permute-start | bytes 393224 | tf_op jit(solution)/shard_map/ppermute | solution.py:37
  32.7 1.5 %collective-permute-start.8 = (bf16[512,128]{1,0:T(8,128)(2,1)S(1)}, bf16[512,128]{1,0:T(8,128)(2,1)S(1)}, u32[]{:S(2)}, u32[]{:S(2)}) collective-permute-start(bf16[512,128]{1,0:T(8,128)(2,1)S(1)} %get-tuple-element.30.refs_3_), channel_id=1, source_target_pairs={{4,0},{13,1},{8,4},{1,5},{12,8},{5,9},{0,12},{9,13},{6,2},{15,3},{... | collective-permute-start | bytes 393224 | tf_op jit(solution)/shard_map/ppermute | solution.py:37
  34.2 0.6 %collective-permute-start.7 = (bf16[512,128]{1,0:T(8,128)(2,1)S(1)}, bf16[512,128]{1,0:T(8,128)(2,1)S(1)}, u32[]{:S(2)}, u32[]{:S(2)}) collective-permute-start(bf16[512,128]{1,0:T(8,128)(2,1)S(1)} %get-tuple-element.29.here_ref), channel_id=1, source_target_pairs={{12,0},{5,1},{0,4},{9,5},{4,8},{13,9},{8,12},{1,13},{14,2},{7,3},{... | collective-permute-start | bytes 393224 | tf_op jit(solution)/shard_map/ppermute | solution.py:37
  34.7 1.9 %collective-permute-done.3.refs_5_ = bf16[512,256]{1,0:T(8,128)(2,1)S(1)} collective-permute-done((bf16[512,256]{1,0:T(8,128)(2,1)S(1)}, bf16[512,256]{1,0:T(8,128)(2,1)S(1)}, u32[]{:S(2)}, u32[]{:S(2)}) %collective-permute-start.3) | collective-permute-done | bytes 262176 | tf_op jit(solution)/shard_map/ppermute | solution.py:37
  36.6 7.5 %collective-permute-start.6 = (bf16[512,128]{1,0:T(8,128)(2,1)S(1)}, bf16[512,128]{1,0:T(8,128)(2,1)S(1)}, u32[]{:S(2)}, u32[]{:S(2)}) collective-permute-start(bf16[512,128]{1,0:T(8,128)(2,1)S(1)} %get-tuple-element.29.here_ref), channel_id=1, source_target_pairs={{4,0},{13,1},{8,4},{1,5},{12,8},{5,9},{0,12},{9,13},{6,2},{15,3},{... | collective-permute-start | bytes 393224 | tf_op jit(solution)/shard_map/ppermute | solution.py:37
  44.1 0.0 collective-permute-done.2.refs_4_
  44.1 0.0 copy-done.1
  44.1 0.0 copy-done.5
  44.1 2.1 %next_part.2 = (f32[512,256]{1,0:T(8,128)S(1)}, f32[512,256]{1,0:T(8,128)S(1)}, f32[512,512]{1,0:T(8,128)}) custom-call(s32[8,8]{1,0:T(8,128)S(1)} %copy-done.4, f32[2]{0:T(128)S(1)} %copy-done.5, bf16[512,1536]{1,0:T(8,128)(2,1)S(1)} %band.1.band_ref.refs_2_, bf16[512,256]{1,0:T(8,128)(2,1)S(1)} %get-tuple-element.24.refs_3_, ...), custom_call_target="tpu_custom_call" | custom-call | flops 402653184 | bytes 3061841 | tf_op jit(solution)/shard_map/next_part/pallas_call | solution.py:199
  46.2 0.0 collective-permute-done.9.refs_5_
  46.2 0.0 collective-permute-done.8.refs_4_
  46.2 2.1 %next_part.3 = (f32[512,128]{1,0:T(8,128)S(1)}, f32[512,128]{1,0:T(8,128)S(1)}, f32[512,512]{1,0:T(8,128)}, f32[512,512]{1,0:T(8,128)}) custom-call(s32[8,8]{1,0:T(8,128)S(1)} %copy-done.4, f32[2]{0:T(128)S(1)} %copy-done.5, bf16[512,1536]{1,0:T(8,128)(2,1)S(1)} %band.1.band_ref.refs_2_, bf16[512,128]{1,0:T(8,128)(2,1)S(1)} %get-tuple-element.30.refs_3_, ...), custom_call_target="tpu_custom_call" | custom-call | flops 201326592 | bytes 2055208 | tf_op jit(solution)/shard_map/next_part/pallas_call | solution.py:199
  48.3 2.4 %collective-permute-done.7.first_ref = bf16[512,128]{1,0:T(8,128)(2,1)S(1)} collective-permute-done((bf16[512,128]{1,0:T(8,128)(2,1)S(1)}, bf16[512,128]{1,0:T(8,128)(2,1)S(1)}, u32[]{:S(2)}, u32[]{:S(2)}) %collective-permute-start.7) | collective-permute-done | bytes 131104 | tf_op jit(solution)/shard_map/ppermute | solution.py:37
  50.7 0.4 begun_part.1.sums_ref
  51.1 0.0 collective-permute-done.6.second_ref
  51.1 1.7 %last_part.1 = (f32[512,512]{1,0:T(8,128)}, f32[512,512]{1,0:T(8,128)}) custom-call(s32[8,8]{1,0:T(8,128)S(1)} %copy-done.4, f32[2]{0:T(128)S(1)} %copy-done.5, bf16[512,1536]{1,0:T(8,128)(2,1)S(1)} %band.1.band_ref.refs_2_, bf16[512,128]{1,0:T(8,128)(2,1)S(1)} %collective-permute-done.6.second_ref, ...), custom_call_target="tpu_custom_call", output_to_operand_aliasing={{0}: (8, {}), {1}: (9, {})} | custom-call | flops 67108864 | bytes 1966080 | tf_op jit(solution)/shard_map/last_part/pallas_call | solution.py:266
  (1 shorter events, 0.0 us)
Async XLA Ops:
  0.6 11.4 %copy-start.6 = (s32[8,16]{1,0:T(8,128)S(1)}, s32[8,16]{1,0:T(8,128)}, u32[]{:S(2)}) copy-start(s32[8,16]{1,0:T(8,128)} %slots_ref.1) | copy-start | bytes 1540
  1.7 12.5 %collective-permute-start.1 = (bf16[512,256]{1,0:T(8,128)(2,1)S(1)}, bf16[512,256]{1,0:T(8,128)(2,1)S(1)}, u32[]{:S(2)}, u32[]{:S(2)}) collective-permute-start(bf16[512,256]{1,0:T(8,128)(2,1)S(1)} %slice.7.here_ref), channel_id=1, source_target_pairs={{12,0},{5,1},{0,4},{9,5},{4,8},{13,9},{8,12},{1,13},{14,2},{7,3},{... | collective-permute-start | bytes 786440 | tf_op jit(solution)/shard_map/ppermute | solution.py:37
  4.8 13.8 %collective-permute-start = (bf16[512,256]{1,0:T(8,128)(2,1)S(1)}, bf16[512,256]{1,0:T(8,128)(2,1)S(1)}, u32[]{:S(2)}, u32[]{:S(2)}) collective-permute-start(bf16[512,256]{1,0:T(8,128)(2,1)S(1)} %slice.7.here_ref), channel_id=1, source_target_pairs={{4,0},{13,1},{8,4},{1,5},{12,8},{5,9},{0,12},{9,13},{6,2},{15,3},{... | collective-permute-start | bytes 786440 | tf_op jit(solution)/shard_map/ppermute | solution.py:37
  6.9 1.2 %copy-start = (f32[512,512]{1,0:T(8,128)S(1)}, f32[512,512]{1,0:T(8,128)}, u32[]{:S(2)}) copy-start(f32[512,512]{1,0:T(8,128)} %now_ref.1) | copy-start | bytes 3145732
  8.1 3.9 %copy-start.3 = (bf16[8,64,1024]{2,1,0:T(8,128)(2,1)S(1)}, bf16[8,64,1024]{2,1,0:T(8,128)(2,1)}, u32[]{:S(2)}) copy-start(bf16[8,64,1024]{2,1,0:T(8,128)(2,1)} %strips_ref) | copy-start | bytes 3145732
  8.2 10.4 %copy-start.2 = (f32[512,512]{1,0:T(8,128)S(1)}, f32[512,512]{1,0:T(8,128)}, u32[]{:S(2)}) copy-start(f32[512,512]{1,0:T(8,128)} %prev_ref.1) | copy-start | bytes 3145732
  8.2 10.4 %copy-start.4 = (s32[8,8]{1,0:T(8,128)S(1)}, s32[8,8]{1,0:T(8,128)}, u32[]{:S(2)}) copy-start(s32[8,8]{1,0:T(8,128)} %mask_ref.5) | copy-start | bytes 772
  8.2 17.1 %collective-permute-start.5 = (bf16[512,256]{1,0:T(8,128)(2,1)S(1)}, bf16[512,256]{1,0:T(8,128)(2,1)S(1)}, u32[]{:S(2)}, u32[]{:S(2)}) collective-permute-start(bf16[512,256]{1,0:T(8,128)(2,1)S(1)} %round_part.1.here_ref), channel_id=1, source_target_pairs={{12,0},{5,1},{0,4},{9,5},{4,8},{13,9},{8,12},{1,13},{14,2},{7,3},{... | collective-permute-start | bytes 786440 | tf_op jit(solution)/shard_map/ppermute | solution.py:37
  8.2 20.7 %collective-permute-start.4 = (bf16[512,256]{1,0:T(8,128)(2,1)S(1)}, bf16[512,256]{1,0:T(8,128)(2,1)S(1)}, u32[]{:S(2)}, u32[]{:S(2)}) collective-permute-start(bf16[512,256]{1,0:T(8,128)(2,1)S(1)} %round_part.1.here_ref), channel_id=1, source_target_pairs={{4,0},{13,1},{8,4},{1,5},{12,8},{5,9},{0,12},{9,13},{6,2},{15,3},{... | collective-permute-start | bytes 786440 | tf_op jit(solution)/shard_map/ppermute | solution.py:37
  19.8 16.9 %collective-permute-start.3 = (bf16[512,256]{1,0:T(8,128)(2,1)S(1)}, bf16[512,256]{1,0:T(8,128)(2,1)S(1)}, u32[]{:S(2)}, u32[]{:S(2)}) collective-permute-start(bf16[512,256]{1,0:T(8,128)(2,1)S(1)} %get-tuple-element.24.refs_3_), channel_id=1, source_target_pairs={{12,0},{5,1},{0,4},{9,5},{4,8},{13,9},{8,12},{1,13},{14,2},{7,3},{... | collective-permute-start | bytes 786440 | tf_op jit(solution)/shard_map/ppermute | solution.py:37
  22.5 21.5 %collective-permute-start.2 = (bf16[512,256]{1,0:T(8,128)(2,1)S(1)}, bf16[512,256]{1,0:T(8,128)(2,1)S(1)}, u32[]{:S(2)}, u32[]{:S(2)}) collective-permute-start(bf16[512,256]{1,0:T(8,128)(2,1)S(1)} %get-tuple-element.24.refs_3_), channel_id=1, source_target_pairs={{4,0},{13,1},{8,4},{1,5},{12,8},{5,9},{0,12},{9,13},{6,2},{15,3},{... | collective-permute-start | bytes 786440 | tf_op jit(solution)/shard_map/ppermute | solution.py:37
  28.9 15.2 %copy-start.1 = (f32[512,512]{1,0:T(8,128)S(1)}, f32[512,512]{1,0:T(8,128)}, u32[]{:S(2)}) copy-start(f32[512,512]{1,0:T(8,128)} %now_ref.1) | copy-start | bytes 3145732
  28.9 15.2 %copy-start.5 = (f32[2]{0:T(128)S(1)}, f32[2]{0:T(128)}, u32[]{:S(2)}) copy-start(f32[2]{0:T(128)} %coeffs_ref.1) | copy-start | bytes 28
  30.1 16.1 %collective-permute-start.9 = (bf16[512,128]{1,0:T(8,128)(2,1)S(1)}, bf16[512,128]{1,0:T(8,128)(2,1)S(1)}, u32[]{:S(2)}, u32[]{:S(2)}) collective-permute-start(bf16[512,128]{1,0:T(8,128)(2,1)S(1)} %get-tuple-element.30.refs_3_), channel_id=1, source_target_pairs={{12,0},{5,1},{0,4},{9,5},{4,8},{13,9},{8,12},{1,13},{14,2},{7,3},{... | collective-permute-start | bytes 393224 | tf_op jit(solution)/shard_map/ppermute | solution.py:37
  32.7 13.5 %collective-permute-start.8 = (bf16[512,128]{1,0:T(8,128)(2,1)S(1)}, bf16[512,128]{1,0:T(8,128)(2,1)S(1)}, u32[]{:S(2)}, u32[]{:S(2)}) collective-permute-start(bf16[512,128]{1,0:T(8,128)(2,1)S(1)} %get-tuple-element.30.refs_3_), channel_id=1, source_target_pairs={{4,0},{13,1},{8,4},{1,5},{12,8},{5,9},{0,12},{9,13},{6,2},{15,3},{... | collective-permute-start | bytes 393224 | tf_op jit(solution)/shard_map/ppermute | solution.py:37
  34.2 16.5 %collective-permute-start.7 = (bf16[512,128]{1,0:T(8,128)(2,1)S(1)}, bf16[512,128]{1,0:T(8,128)(2,1)S(1)}, u32[]{:S(2)}, u32[]{:S(2)}) collective-permute-start(bf16[512,128]{1,0:T(8,128)(2,1)S(1)} %get-tuple-element.29.here_ref), channel_id=1, source_target_pairs={{12,0},{5,1},{0,4},{9,5},{4,8},{13,9},{8,12},{1,13},{14,2},{7,3},{... | collective-permute-start | bytes 393224 | tf_op jit(solution)/shard_map/ppermute | solution.py:37
  36.6 14.5 %collective-permute-start.6 = (bf16[512,128]{1,0:T(8,128)(2,1)S(1)}, bf16[512,128]{1,0:T(8,128)(2,1)S(1)}, u32[]{:S(2)}, u32[]{:S(2)}) collective-permute-start(bf16[512,128]{1,0:T(8,128)(2,1)S(1)} %get-tuple-element.29.here_ref), channel_id=1, source_target_pairs={{4,0},{13,1},{8,4},{1,5},{12,8},{5,9},{0,12},{9,13},{6,2},{15,3},{... | collective-permute-start | bytes 393224 | tf_op jit(solution)/shard_map/ppermute | solution.py:37
